TPU v7x, 32 devices: a whole 2x2x4 slice. The times are simulated.
32 devices in a mesh: clip: 16 (over z, x, core), tm: 2 (over y).
Axes of the slice: x: 2, y: 2, z: 4, core: 2. Of those that a mesh axis runs over, the one named last changes fastest.
Arguments:
- inputs: float32 [32, 2048, 512], P('clip', 'tm'), may hold values from -6 to 6
- band_ids: int32 [32], P('clip'), may hold values from 0 to 3
- offsets: int32 [32], P('clip'), may hold values from 0 to 511
- conv_weight: float32 [7, 512], replicated, may hold values from -2 to 2
- conv_bias: float32 [512], replicated, may hold values from -3 to 3
- scale_table: float32 [4, 512], replicated, may hold values from 0.25 to 1.75
- shift_table: float32 [4, 512], replicated, may hold values from -3 to 3
- up_weight: float32 [512, 1536], replicated, may hold values from -0.25 to 0.25
- up_bias: float32 [1536], replicated, may hold values from -3 to 3
- down_weight: float32 [1536, 512], replicated, may hold values from -0.15625 to 0.15625
- down_bias: float32 [512], replicated, may hold values from -2 to 2
- layer_scale: float32 [512], replicated, may hold values from 0.25 to 1.75
- head_weight: float32 [512, 1282], replicated, may hold values from -0.1875 to 0.1875
- head_bias: float32 [1282], replicated, may hold values from 1.5 to 3.5
- wave_cotangent: float32 [32, 655360], P('clip', 'tm'), may hold values from -6 to 6
Outputs:
- waveform: float32 [32, 655360], P('clip', 'tm')
- grad_inputs: float32 [32, 2048, 512], P('clip', 'tm')
- grad_conv_weight: float32 [7, 512], replicated
- grad_conv_bias: float32 [512], replicated
- grad_scale_table: float32 [4, 512], replicated
- grad_shift_table: float32 [4, 512], replicated
- grad_up_weight: float32 [512, 1536], replicated
- grad_up_bias: float32 [1536], replicated
- grad_down_weight: float32 [1536, 512], replicated
- grad_down_bias: float32 [512], replicated
- grad_layer_scale: float32 [512], replicated
- grad_head_weight: float32 [512, 1282], replicated
- grad_head_bias: float32 [1282], replicated
All inputs are finite; a program needn't handle non-finite values.
Results may differ from a plain program's by a relative error of at most 0.0003.
Values sent between devices are 32-bit elements; how exact they have to be, the bound alone decides.
No kernel may reach another device: no remote copies, remote signals or barrier semaphores. Data moves between devices by JAX's collectives and lax.ppermute only.
A program may use at most 192 MiB of HBM per device.

v0:
```python
import functools

import jax
import jax.numpy as jnp
import ml_dtypes
import numpy as np
from jax import lax
from jax.experimental import pallas as pl
from jax.experimental.pallas import tpu as pltpu
from jax.sharding import PartitionSpec as P

KERNEL = 7
CLASSES = ((1, 4), (2, 3), (0,))
F32 = jnp.float32
BF16 = jnp.bfloat16
LANES = 128
PAIRS = 128
ROWS = 2 * PAIRS
VMEM = 60 * 2**20
UP_PARTS = ((1024, 0), (512, 2))
HEAD_ROWS = 704
SDS = jax.ShapeDtypeStruct

SIN_POLY = (0.999999996, -0.166666580, 8.33305023e-03, -1.98090119e-04, 2.60507821e-06)
COS_POLY = (1.0, -0.499999994, 4.16666361e-02, -1.38883598e-03, 2.47600798e-05, -2.60500270e-07)

NN = (((1,), (0,)), ((), ()))
NT = (((1,), (1,)), ((), ()))


def split(x):
    high = x.astype(BF16)
    return high, (x - high.astype(F32)).astype(BF16)


def dot(a, b, dims=NN):
    return lax.dot_general(a, b, dims, preferred_element_type=F32)


def dot3(a, b, dims=NN):
    return dot(a[0], b[0], dims) + (dot(a[0], b[1], dims) + dot(a[1], b[0], dims))


def fold8(x):
    return jnp.sum(x.reshape(x.shape[0] // 8, 8, x.shape[1]), axis=0)


def np_split(x):
    high = x.astype(np.float32).astype(ml_dtypes.bfloat16)
    return high, (x - high.astype(np.float64)).astype(ml_dtypes.bfloat16)


@functools.lru_cache(None)
def tables(nfft):
    fifth, half, hop = nfft // 5, nfft // 2, nfft // 4
    bins = np.arange(1, half)
    first, second = (np.concatenate([bins[bins % 5 == r] for r in rs]) for rs in CLASSES[:2])
    zero = np.arange(0, half, 5)
    n0 = np.arange(fifth)

    def paired(ks, residue):
        sign = np.where(ks % 5 == residue, 1.0, -1.0)[:, None]
        turn = 2 * np.pi * ((sign * ks[:, None] * n0[None]) % nfft) / nfft
        weight = 2.0 / nfft
        real = np.concatenate([weight * np.cos(turn), weight * np.sin(turn)], 1)
        imag = np.concatenate([-sign * weight * np.sin(turn), sign * weight * np.cos(turn)], 1)
        return np.concatenate([real, imag], 0)

    turn = 2 * np.pi * ((zero[:, None] * n0[None]) % nfft) / nfft
    weight = np.where(zero == 0, 1.0, 2.0)[:, None] / nfft
    real, imag = weight * np.cos(turn), -weight * np.sin(turn)
    imag[0] = np.cos(np.pi * n0) / nfft
    transforms = [np_split(t) for t in (paired(first, 1), paired(second, 2), np.concatenate([real, imag], 0))]
    n = np.arange(nfft)
    window = 0.5 - 0.5 * np.cos(2 * np.pi * n / nfft)
    windows = np.stack([window, np.roll(window, hop)]).astype(np.float32)
    squares = np.cumsum((window**2).reshape(4, hop), axis=0)
    inverse = np.tile(1.0 / np.maximum(squares, 1.0), (1, 2)).astype(np.float32)
    turns = np.zeros(nfft)
    place = 0
    for ks in (first, second, zero):
        turns[place + len(ks) : place + 2 * len(ks)] = -(np.pi / 2) * (ks % 4)
        place += 2 * len(ks)
    return transforms, windows, inverse, turns.astype(np.float32)[None]


def class_places(nfft):
    length, places, at = nfft // 10, [], 0
    for residues in CLASSES:
        for offset in (0, nfft // 2 + 1):
            for r in residues:
                places.append((at, offset + r))
                at += length
    return places


def sin_cos(x):
    turns = jnp.round(x * np.float32(0.5 / np.pi))
    h = x * 0.5 - turns * np.float32(3.140625)
    h = h - turns * np.float32(9.67502593994140625e-4)
    h = h - turns * np.float32(1.509957990978376432e-7)
    z = h * h
    s = np.float32(SIN_POLY[-1])
    for c in SIN_POLY[-2::-1]:
        s = s * z + np.float32(c)
    s = s * h
    cosine = np.float32(COS_POLY[-1])
    for c in COS_POLY[-2::-1]:
        cosine = cosine * z + np.float32(c)
    twice = s + s
    return twice * cosine, 1.0 - twice * s


def fifths():
    a = 2 * np.pi / 5
    return [np.float32(v) for v in (np.cos(a), np.cos(2 * a), np.sin(a), np.sin(2 * a))]


def inverse_envelope(first_pair, offset, table_ref, tile, rows):
    lane = tile * LANES + lax.broadcasted_iota(jnp.int32, (rows, LANES), 1)
    row = lax.broadcasted_iota(jnp.int32, (rows, LANES), 0)
    half = table_ref.shape[1] // 2
    since = 2 * (first_pair + row) + (lane >= half).astype(jnp.int32) - offset
    value = jnp.where(since < 0, 1.0, 1.0)
    for i in range(4):
        value = jnp.where(since >= i, table_ref[i : i + 1, tile * LANES : (tile + 1) * LANES], value)
    return value


def head_kernel(
    bands,
    offsets,
    x_ref,
    x_up,
    x_down,
    edge_ref,
    cot_ref,
    cot_down,
    cot_edge,
    conv_w,
    conv_b,
    scale_t,
    shift_t,
    up_w,
    up_b,
    down_w,
    down_b,
    layer_scale,
    head_wt,
    head_b,
    turns,
    t1h,
    t1l,
    t2h,
    t2l,
    t0h,
    t0l,
    windows,
    inverse,
    o_norm,
    o_istd,
    o_adt_h,
    o_adt_l,
    o_act_h,
    o_act_l,
    o_slope,
    o_spec,
    o_gm,
    o_gb_h,
    o_gb_l,
    o_gbt_h,
    o_gbt_l,
    o_keep,
    o_send,
    o_small,
    up_h,
    up_l,
    down_h,
    down_l,
    head_h,
    head_l,
    head_bias,
    ext_w,
    head4,
    bias4,
    pad4,
    nrm4,
    istd1,
    gs5,
    gm4,
    gl_h,
    gl_l,
    acc_ghw,
    acc_ghb,
    acc_ghwe,
    acc_ghbe,
    acc_gls,
    acc_gmb,
):
    clip, blk = pl.program_id(0), pl.program_id(1)
    clips, blks = pl.num_programs(0), pl.num_programs(1)
    width = x_ref.shape[2]
    frames = blks * ROWS
    tiles = width // LANES
    nfft = turns.shape[1]
    half = nfft // 2
    tm = lax.axis_index("tm")
    band = bands[clip]
    local = offsets[clip] - tm * frames
    rows8 = edge_ref.shape[1]
    places = class_places(nfft)

    @pl.when((clip == 0) & (blk == 0))
    def _():
        up_h[...], up_l[...] = split(up_w[...])
        down_h[...], down_l[...] = split(down_w[...])
        for t in range(tiles):
            head4[t, 0 : nfft + 2, :] = head_wt[:, t * LANES : (t + 1) * LANES]
        bias = head_b[...].reshape(1, nfft + 2)
        for c in range(0, nfft, LANES):
            bias4[c : c + LANES, :] = jnp.broadcast_to(bias[:, c : c + LANES], (LANES, LANES)).T
        for c in (nfft, nfft + 1):
            bias4[c : c + 1, :] = jnp.broadcast_to(bias[:, c : c + 1], (1, LANES))
        for at, first in places:
            rows = jnp.concatenate([head4[t, pl.ds(first, LANES, stride=5), :] for t in range(tiles)], 1)
            head_h[at : at + LANES, :], head_l[at : at + LANES, :] = split(rows)
            moved = bias4[pl.ds(first, LANES, stride=5), :].T[0:1, :]
            head_bias[0:1, at : at + LANES] = moved
            head_bias[1:2, at : at + LANES] = moved + turns[:, at : at + LANES]
        ext_w[0:1, :] = head_wt[half : half + 1, :]
        ext_w[1:2, :] = head_wt[nfft + 1 : nfft + 2, :]
        ext_w[2:8, :] = jnp.zeros((6, width), F32)
        for ref in (acc_ghw, acc_ghb, acc_ghwe, acc_ghbe, acc_gls, acc_gmb):
            ref[...] = jnp.zeros_like(ref)

    base = pl.multiple_of(blk * ROWS, ROWS)

    def masked(value, first):
        row = first + lax.broadcasted_iota(jnp.int32, value.shape, 0)
        return jnp.where(row >= local, value, 0.0)

    before = masked(jnp.where(blk == 0, jnp.where(tm > 0, edge_ref[0], 0.0), x_up[0]), base - rows8)
    after = masked(jnp.where(blk == blks - 1, jnp.where(tm > 0, 0.0, edge_ref[0]), x_down[0]), base + ROWS)
    middle = masked(x_ref[0], base)
    for t in range(tiles):
        lanes = slice(t * LANES, (t + 1) * LANES)
        pad4[t, 0:rows8, :] = before[:, lanes]
        pad4[t, rows8 : rows8 + ROWS, :] = middle[:, lanes]
        pad4[t, rows8 + ROWS :, :] = after[:, lanes]
    bias = conv_b[...].reshape(1, width)
    chunk = 64
    for r in range(0, ROWS, chunk):
        parts = []
        for t in range(tiles):
            lanes = slice(t * LANES, (t + 1) * LANES)
            total = bias[:, lanes]
            for k in range(KERNEL):
                first = r + rows8 - KERNEL // 2 + k
                total = total + pad4[t, first : first + chunk, :] * conv_w[k : k + 1, lanes]
            parts.append(total)
        mean = jnp.sum(sum(parts[1:], parts[0]), axis=1, keepdims=True) * (1.0 / width)
        parts = [p - mean for p in parts]
        squares = [p * p for p in parts]
        variance = jnp.sum(sum(squares[1:], squares[0]), axis=1, keepdims=True) * (1.0 / width)
        istd = lax.rsqrt(variance + 1e-6)
        for t in range(tiles):
            nrm4[t, r : r + chunk, :] = parts[t] * istd
        istd1[r : r + chunk, :] = jnp.broadcast_to(istd, (chunk, LANES))

    def by_parity(ref, first):
        return jnp.concatenate(
            [
                jnp.concatenate([ref[t, pl.ds(first + par, PAIRS, stride=2), :] for t in range(tiles)], 1)
                for par in range(2)
            ],
            0,
        )

    normed = by_parity(nrm4, 0)
    o_norm[...] = normed
    for par in range(2):
        o_istd[par * PAIRS : (par + 1) * PAIRS, :] = istd1[pl.ds(par, PAIRS, stride=2), :]
    adapted = normed * scale_t[pl.ds(band, 1), :] + shift_t[pl.ds(band, 1), :]
    ad = split(adapted)
    o_adt_h[...], o_adt_l[...] = ad[0].T, ad[1].T

    first_pair = pl.multiple_of(blk * PAIRS, PAIRS)
    wave_tiles = gs5.shape[0]
    for t in range(wave_tiles):
        lanes = slice(t * LANES, (t + 1) * LANES)
        stride = clips * wave_tiles
        value = cot_ref[pl.ds(clips * t + clip, PAIRS, stride=stride), :]
        gs5[t, 0:PAIRS, :] = value * inverse_envelope(first_pair, local, inverse, t, PAIRS)
        value = cot_down[pl.ds(clips * t + clip, 8, stride=stride), :]
        value = jnp.where(blk == blks - 1, jnp.where(tm > 0, 0.0, cot_edge[0, :, lanes]), value)
        gs5[t, PAIRS : PAIRS + 8, :] = value * inverse_envelope(first_pair + PAIRS, local, inverse, t, 8)
    now, one, two = ([gs5[t, d : d + PAIRS, :] for t in range(wave_tiles)] for d in range(3))
    mid = wave_tiles // 2
    right = lax.broadcasted_iota(jnp.int32, (PAIRS, LANES), 1) >= LANES // 2
    odd = two[:mid] + [jnp.where(right, now[mid], two[mid])] + now[mid + 1 :] + one
    c1, c2, s1, s2 = fifths()
    folded = []
    for par, segment in enumerate((now + one, odd)):
        seg = [v * windows[par : par + 1, t * LANES : (t + 1) * LANES] for t, v in enumerate(segment)]
        v = [jnp.concatenate(seg[2 * j : 2 * j + 2], 1) for j in range(5)]
        p14, m41, p23, m32 = v[1] + v[4], v[4] - v[1], v[2] + v[3], v[3] - v[2]
        folded.append(
            (
                v[0] + p14 + p23,
                v[0] + c1 * p14 + c2 * p23,
                s1 * m41 + s2 * m32,
                v[0] + c2 * p14 + c1 * p23,
                s2 * m41 - s1 * m32,
            )
        )
    f0, fa, fb, fc, fd = (jnp.concatenate([e, o], 0) for e, o in zip(*folded))
    spectrum_grads = (
        dot3(split(jnp.concatenate([fa, fb], 1)), (t1h[...], t1l[...]), NT),
        dot3(split(jnp.concatenate([fc, fd], 1)), (t2h[...], t2l[...]), NT),
        dot3(split(f0), (t0h[...], t0l[...]), NT),
    )

    hidden = up_h.shape[1]
    step = 256
    up_bias = up_b[...].reshape(1, hidden)
    for j in range(hidden // step):
        cols = slice(j * step, (j + 1) * step)
        upward = dot3(ad, (up_h[:, cols], up_l[:, cols])) + up_bias[:, cols]
        cdf = 0.5 + 0.5 * lax.erf(upward * np.float32(0.7071067811865476))
        density = jnp.exp(upward * upward * -0.5) * np.float32(0.3989422804014327)
        o_slope[:, cols] = cdf + upward * density
        o_act_h[:, cols], o_act_l[:, cols] = split(upward * cdf)
    branch = dot3((o_act_h[...], o_act_l[...]), (down_h[...], down_l[...])) + down_b[...].reshape(1, width)
    scale = layer_scale[...].reshape(1, width)
    residual = by_parity(pad4, rows8) + scale * branch
    res = split(residual)
    res_t = res[0].T, res[1].T

    bias = head_b[...].reshape(1, nfft + 2)
    ext = split(ext_w[...])
    ext_logits = dot3(ext, res, NT)
    lane = lax.broadcasted_iota(jnp.int32, (1, ROWS), 1)
    ext_frame = base + jnp.where(lane < PAIRS, 2 * lane, 2 * (lane - PAIRS) + 1)
    ext_present = ext_frame >= local

    def magnitudes(logits, present):
        raw = jnp.where(present, jnp.exp(logits), 0.0)
        squashed = jnp.tanh(raw * np.float32(0.01))
        return 100.0 * squashed, raw * (1.0 - squashed * squashed)

    ext_mag, ext_slope = magnitudes(ext_logits[0:1] + bias[:, half : half + 1], ext_present)
    ext_sin, ext_cos = sin_cos(ext_logits[1:2] + bias[:, nfft + 1 : nfft + 2])
    ext_real = ext_mag * ext_cos
    ext_imag = ext_mag * ext_sin
    ext_real_col = jnp.concatenate([ext_real, jnp.zeros((7, ROWS), F32)], 0).T[:, 0:1]

    row = lax.broadcasted_iota(jnp.int32, (PAIRS, 1), 0)
    at = 0
    for index, grads in enumerate(spectrum_grads):
        n = grads.shape[1] // 2
        cols = slice(at, at + 2 * n)
        logits = dot3(res, (head_h[cols, :], head_l[cols, :]), NT)
        for par in range(2):
            rows = slice(par * PAIRS, (par + 1) * PAIRS)
            present = base + 2 * row + par >= local
            value = logits[rows] + head_bias[par : par + 1, cols]
            magnitude, slope = magnitudes(value[:, :n], present)
            sine, cosine = sin_cos(value[:, n:])
            real, imag = magnitude * cosine, magnitude * sine
            g_real, g_imag = grads[rows, :n], grads[rows, n:]
            if index == 2:
                corner = lax.broadcasted_iota(jnp.int32, (PAIRS, n), 1) == 0
                shown = jnp.where(corner, ext_real_col[rows], imag)
                g_imag = jnp.where(corner, 0.0, g_imag)
            else:
                shown = imag
            o_spec[rows, at : at + n] = real
            o_spec[rows, at + n : at + 2 * n] = shown
            g_mag = slope * (g_real * cosine + g_imag * sine)
            g_ang = g_imag * real - g_real * imag
            gl = jnp.concatenate([g_mag, g_ang], 1)
            acc_ghb[:, cols] += fold8(gl)
            gl_h[rows, cols], gl_l[rows, cols] = split(gl)
        at += 2 * n

    corner_t = spectrum_grads[2][:, spectrum_grads[2].shape[1] // 2 :].T
    ext_g = corner_t[0:1, :]
    ext_grads = jnp.concatenate(
        [ext_slope * ext_g * ext_cos, -ext_g * ext_imag, jnp.zeros((6, ROWS), F32)], 0
    )
    acc_ghbe[...] += ext_grads
    acc_ghwe[...] += dot3(split(ext_grads), res)
    gl = (gl_h[...], gl_l[...])
    ext_cols = ext_grads.T
    grad_mixed = (
        dot3(gl, (head_h[...], head_l[...]))
        + ext_cols[:, 0:1] * ext_w[0:1, :]
        + ext_cols[:, 1:2] * ext_w[1:2, :]
    )
    acc_ghw[...] += dot3(res_t, gl)
    acc_gls[...] += fold8(grad_mixed * branch)
    acc_gmb[...] += fold8(grad_mixed)
    for par in range(2):
        rows = slice(par * PAIRS, (par + 1) * PAIRS)
        for t in range(tiles):
            gm4[t, pl.ds(par, PAIRS, stride=2), :] = grad_mixed[rows, t * LANES : (t + 1) * LANES]
    for t in range(tiles):
        o_gm[:, t * LANES : (t + 1) * LANES] = gm4[t]
    grad_branch = grad_mixed * scale
    gb = split(grad_branch)
    o_gb_h[...], o_gb_l[...] = gb
    o_gbt_h[...], o_gbt_l[...] = gb[0].T, gb[1].T

    @pl.when((clip == clips - 1) & (blk == blks - 1))
    def _():
        total = jnp.sum(acc_ghb[...], axis=0, keepdims=True)
        for at, first in places:
            for t in range(tiles):
                block = acc_ghw[t * LANES : (t + 1) * LANES, at : at + LANES]
                head4[t, pl.ds(first, LANES, stride=5), :] = block.T
            block = jnp.broadcast_to(total[:, at : at + LANES], (LANES, LANES))
            bias4[pl.ds(first, LANES, stride=5), :] = block.T
        ext_sums = jnp.sum(acc_ghbe[...], axis=1, keepdims=True)
        for i, c in enumerate((half, nfft + 1)):
            for t in range(tiles):
                head4[t, c : c + 1, :] = acc_ghwe[i : i + 1, t * LANES : (t + 1) * LANES]
            bias4[c : c + 1, :] = jnp.broadcast_to(ext_sums[i : i + 1], (1, LANES))
        core = lax.axis_index("clip") % 2
        for here, first in ((core == 0, 0), (core == 1, half + 1)):

            @pl.when(here)
            def _(first=first):
                for t in range(tiles):
                    lanes = slice(t * LANES, (t + 1) * LANES)
                    for ref, at in ((o_keep, first), (o_send, half + 1 - first)):
                        ref[0 : half + 1, lanes] = head4[t, at : at + half + 1, :]
                        ref[half + 1 :, lanes] = jnp.zeros((ref.shape[0] - half - 1, LANES), F32)

        o_small[...] = jnp.zeros_like(o_small)
        for c in range(0, nfft, LANES):
            o_small[0:1, c : c + LANES] = bias4[c : c + LANES, :].T[0:1, :]
        o_small[0:1, nfft : nfft + 2] = jnp.concatenate(
            [bias4[nfft : nfft + 1, 0:1], bias4[nfft + 1 : nfft + 2, 0:1]], 1
        )
        o_small[1:2, :width] = jnp.sum(acc_gls[...], axis=0, keepdims=True)
        o_small[2:3, :width] = jnp.sum(acc_gmb[...], axis=0, keepdims=True) * scale


def whole(shape):
    return pl.BlockSpec(shape, lambda *_: (0,) * len(shape))


def fixed(shape):
    return pl.BlockSpec(shape, lambda *_: (0,) * len(shape), pipeline_mode=pl.Buffered(1))


def row_halves(blks, rows, rows8, width, clip=None):
    per, last = rows // rows8, blks * rows // rows8 - 1
    places = [
        (rows, lambda j: j),
        (rows8, lambda j: jnp.maximum(j * per - 1, 0)),
        (rows8, lambda j: jnp.minimum(j * per + per, last)),
    ]
    if clip is None:
        return [pl.BlockSpec((1, n, width), lambda i, j, *_, f=f: (i, f(j), 0)) for n, f in places]
    return [pl.BlockSpec((1, n, width), lambda j, *_, f=f: (clip, f(j), 0)) for n, f in places]


def run_head(bands, offsets, x, edge, cot, cot_edge, weights, turns, consts):
    clips, frames, width = x.shape
    blks = frames // ROWS
    count = clips * frames
    hidden = weights[4].shape[1]
    nfft = turns.shape[1]
    block = lambda i, j, *_: (i * blks + j, 0)
    column = lambda i, j, *_: (0, i * blks + j)
    per_clip = lambda shape: pl.BlockSpec((1,) + shape, lambda i, j, *_: (i, 0, 0))
    in_specs = row_halves(blks, ROWS, edge.shape[1], width)
    in_specs += [per_clip(edge.shape[1:])]
    operands = list(weights) + [turns] + list(consts)
    rows = cot.shape[0] // blks
    few = rows * 8 // PAIRS
    per, last = rows // few, cot.shape[0] // few - 1
    in_specs += [
        pl.BlockSpec((rows, LANES), lambda i, j, *_: (j, 0)),
        pl.BlockSpec((few, LANES), lambda i, j, *_: (jnp.minimum(j * per + per, last), 0)),
        per_clip(cot_edge.shape[1:]),
    ]
    in_specs += [fixed(v.shape) for v in operands]
    row_out = lambda n, dtype: (SDS((count, n), dtype), pl.BlockSpec((ROWS, n), block))
    col_out = (SDS((width, count), BF16), pl.BlockSpec((width, ROWS), column))
    outs = [
        row_out(width, F32),
        row_out(LANES, F32),
        col_out,
        col_out,
        row_out(hidden, BF16),
        row_out(hidden, BF16),
        row_out(hidden, F32),
        row_out(nfft, F32),
        row_out(width, F32),
        row_out(width, BF16),
        row_out(width, BF16),
        col_out,
        col_out,
        (SDS((HEAD_ROWS + hidden // 2, width), F32), whole((HEAD_ROWS, width))),
        (SDS((HEAD_ROWS + hidden // 2, width), F32), whole((HEAD_ROWS, width))),
        (SDS((8, hidden), F32), whole((8, hidden))),
    ]
    wave_tiles = nfft // 2 // LANES
    tiles = width // LANES
    scratch = [pltpu.VMEM((width, hidden), BF16)] * 2 + [pltpu.VMEM((hidden, width), BF16)] * 2
    scratch += [
        pltpu.VMEM((nfft, width), BF16),
        pltpu.VMEM((nfft, width), BF16),
        pltpu.VMEM((2, nfft), F32),
        pltpu.VMEM((8, width), F32),
        pltpu.VMEM((tiles, nfft + 8, LANES), F32),
        pltpu.VMEM((nfft + 8, LANES), F32),
        pltpu.VMEM((tiles, ROWS + 2 * edge.shape[1], LANES), F32),
        pltpu.VMEM((tiles, ROWS, LANES), F32),
        pltpu.VMEM((ROWS, LANES), F32),
        pltpu.VMEM((wave_tiles, PAIRS + 8, LANES), F32),
        pltpu.VMEM((tiles, ROWS, LANES), F32),
        pltpu.VMEM((ROWS, nfft), BF16),
        pltpu.VMEM((ROWS, nfft), BF16),
        pltpu.VMEM((width, nfft), F32),
        pltpu.VMEM((8, nfft), F32),
        pltpu.VMEM((8, width), F32),
        pltpu.VMEM((8, ROWS), F32),
        pltpu.VMEM((8, width), F32),
        pltpu.VMEM((8, width), F32),
    ]
    return pl.pallas_call(
        head_kernel,
        grid_spec=pltpu.PrefetchScalarGridSpec(
            num_scalar_prefetch=2,
            grid=(clips, blks),
            in_specs=in_specs,
            out_specs=[s for _, s in outs],
            scratch_shapes=scratch,
        ),
        out_shape=[s for s, _ in outs],
        compiler_params=pltpu.CompilerParams(vmem_limit_bytes=VMEM),
        cost_estimate=pl.CostEstimate(flops=80_000_000_000, bytes_accessed=90_000_000, transcendentals=0),
        name="head",
    )(bands, offsets, x, x, x, edge, cot, cot, cot_edge, *operands)


def down_kernel(gbt_h, gbt_l, act_h, act_l, *refs):
    o_keep, o_send, acc, keep, send, sems = refs[-6:]
    step = pl.program_id(0)

    @pl.when(step == 0)
    def _():
        acc[...] = jnp.zeros_like(acc)

    acc[...] += dot3((gbt_h[...], gbt_l[...]), (act_h[...], act_l[...]))

    @pl.when(step == pl.num_programs(0) - 1)
    def _():
        core = lax.axis_index("clip") % 2
        rows = keep.shape[0]
        copies = []
        for i, (ref, out, half) in enumerate(((keep, o_keep, core), (send, o_send, 1 - core))):
            mine = pl.ds(pl.multiple_of(half * rows, rows), rows)
            ref[...] = acc[:, mine].T
            above = out.shape[0] - rows
            copies.append(pltpu.make_async_copy(ref, out.at[pl.ds(above, rows), :], sems.at[i]))
            copies[-1].start()
        for copy in copies:
            copy.wait()


def run_down(gbt, act, keep, send):
    width, count = gbt[0].shape
    hidden = act[0].shape[1]
    rows = 512
    any_spec = pl.BlockSpec(memory_space=pl.ANY)
    half = pltpu.VMEM((hidden // 2, width), F32)
    return pl.pallas_call(
        down_kernel,
        grid=(count // rows,),
        in_specs=[pl.BlockSpec((width, rows), lambda i: (0, i))] * 2
        + [pl.BlockSpec((rows, hidden), lambda i: (i, 0))] * 2
        + [any_spec] * 2,
        out_specs=[any_spec] * 2,
        out_shape=[SDS(keep.shape, F32), SDS(send.shape, F32)],
        input_output_aliases={4: 0, 5: 1},
        scratch_shapes=[pltpu.VMEM((width, hidden), F32), half, half, pltpu.SemaphoreType.DMA((2,))],
        compiler_params=pltpu.CompilerParams(vmem_limit_bytes=VMEM),
        cost_estimate=pl.CostEstimate(flops=10_000_000_000, bytes_accessed=20_000_000, transcendentals=0),
        name="down_grads",
    )(*gbt, *act, keep, send)


def up_kernel(gb_h, gb_l, slope, adt_h, adt_l, down_w, *refs):
    o_keep, o_send, o_gub, o_gu_h, o_gu_l, dw_h, dw_l, acc, acc_gub = refs[-9:]
    step = pl.program_id(0)
    hidden = slope.shape[1]

    @pl.when(step == 0)
    def _():
        dw_h[...], dw_l[...] = split(down_w[...])
        acc[...] = jnp.zeros_like(acc)
        acc_gub[...] = jnp.zeros_like(acc_gub)

    cols = 512
    for j in range(hidden // cols):
        part = slice(j * cols, (j + 1) * cols)
        gu = dot3((gb_h[...], gb_l[...]), (dw_h[part, :], dw_l[part, :]), NT) * slope[:, part]
        acc_gub[:, part] += fold8(gu)
        gs = split(gu)
        o_gu_h[:, part], o_gu_l[:, part] = gs
        acc[:, part] += dot3((adt_h[...], adt_l[...]), gs)

    @pl.when(step == pl.num_programs(0) - 1)
    def _():
        o_gub[...] = jnp.sum(acc_gub[...], axis=0, keepdims=True)
        core = lax.axis_index("clip") % 2
        rows = o_keep.shape[0]
        for ref, half in ((o_keep, core), (o_send, 1 - core)):
            ref[...] = acc[:, pl.ds(pl.multiple_of(half * rows, rows), rows)].T


def after(values, operand):
    return lax.optimization_barrier((operand, tuple(values)))[0] if values else operand


def run_up(gb, slope, adt, down_w, size, part, so_far, waits=()):
    count, width = gb[0].shape
    hidden = slope.shape[1]
    rows = 512
    row = lambda i: (i, 0)
    in_specs = [pl.BlockSpec((rows, width), row)] * 2 + [pl.BlockSpec((rows, size), lambda i: (i, part))]
    in_specs += [pl.BlockSpec((width, rows), lambda i: (0, i))] * 2
    in_specs += [pl.BlockSpec((size, width), lambda i: (part, 0), pipeline_mode=pl.Buffered(1))]
    so_far = list(so_far)
    return pl.pallas_call(
        up_kernel,
        grid=(count // rows,),
        in_specs=in_specs + [pl.BlockSpec(memory_space=pl.ANY)] * len(so_far),
        out_specs=[pl.BlockSpec((size // 2, width), lambda i: (part, 0))] * 2
        + [whole((1, size)), pl.BlockSpec((rows, size), row), pl.BlockSpec((rows, size), row)],
        out_shape=[
            SDS((hidden // 2, width), F32),
            SDS((hidden // 2, width), F32),
            SDS((1, size), F32),
            SDS((count, size), BF16),
            SDS((count, size), BF16),
        ],
        input_output_aliases={6 + i: i for i in range(len(so_far))},
        scratch_shapes=[pltpu.VMEM((size, width), BF16)] * 2
        + [pltpu.VMEM((width, size), F32), pltpu.VMEM((8, size), F32)],
        compiler_params=pltpu.CompilerParams(vmem_limit_bytes=VMEM),
        cost_estimate=pl.CostEstimate(flops=10_000_000_000, bytes_accessed=20_000_000, transcendentals=0),
        name="up_grads",
    )(*gb, after(waits, slope), *adt, down_w, *so_far)


def norm_kernel(sizes, clip, bands, *refs):
    gu = refs[: 2 * len(sizes)]
    up_w, norm, istd, scale_t = refs[2 * len(sizes) : 2 * len(sizes) + 4]
    edge_in = refs[2 * len(sizes) + 4] if clip else None
    o_gh, o_edge, o_scale, o_shift, up_h, up_l, nat4, acc_scale, acc_shift = refs[-9:]
    blk, blks = pl.program_id(0), pl.num_programs(0)
    band = bands[clip]
    width = norm.shape[1]
    tiles = width // LANES

    @pl.when(blk == 0)
    def _():
        up_h[...], up_l[...] = split(up_w[...])
        for ref in (o_scale, o_shift, acc_scale, acc_shift):
            ref[...] = jnp.zeros_like(ref)
        if edge_in is not None:
            o_edge[...] = edge_in[...]

    ga, at = None, 0
    for j, hidden in enumerate(sizes):
        cols = slice(at, at + hidden)
        term = dot3((gu[2 * j][...], gu[2 * j + 1][...]), (up_h[:, cols], up_l[:, cols]), NT)
        ga = term if ga is None else ga + term
        at += hidden
    normed = norm[...]
    acc_scale[...] += fold8(ga * normed)
    acc_shift[...] += fold8(ga)
    gn = ga * scale_t[pl.ds(band, 1), :]
    mean = jnp.sum(gn, axis=1, keepdims=True) * (1.0 / width)
    along = jnp.sum(gn * normed, axis=1, keepdims=True) * (1.0 / width)
    gh = istd[:, 0:1] * (gn - mean - normed * along)
    for par in range(2):
        for t in range(tiles):
            nat4[t, pl.ds(par, PAIRS, stride=2), :] = gh[par * PAIRS : (par + 1) * PAIRS, t * LANES : (t + 1) * LANES]
    for t in range(tiles):
        o_gh[:, t * LANES : (t + 1) * LANES] = nat4[t]
    tm = lax.axis_index("tm")
    for here, first in (((tm == 0) & (blk == blks - 1), ROWS - 8), ((tm == 1) & (blk == 0), 0)):

        @pl.when(here)
        def _(first=first):
            for t in range(tiles):
                o_edge[clip, :, t * LANES : (t + 1) * LANES] = nat4[t, first : first + 8, :]

    @pl.when(blk == blks - 1)
    def _():
        o_scale[pl.ds(band, 1), :] = jnp.sum(acc_scale[...], axis=0, keepdims=True)
        o_shift[pl.ds(band, 1), :] = jnp.sum(acc_shift[...], axis=0, keepdims=True)


def run_norm(bands, gus, up_w, norm, istd, scale_t, edge, clip, waits=()):
    clips = edge.shape[0]
    earlier = [edge] if clip else []
    count, width = norm.shape
    blks = count // clips // ROWS
    block = lambda j, *_: (clip * blks + j, 0)
    flat = [v for pair in gus for v in pair]
    in_specs = [pl.BlockSpec((ROWS, v.shape[1]), block) for v in flat]
    in_specs += [fixed(up_w.shape), pl.BlockSpec((ROWS, width), block)]
    in_specs += [pl.BlockSpec((ROWS, LANES), block), fixed(scale_t.shape)]
    in_specs += [fixed(v.shape) for v in earlier]
    return pl.pallas_call(
        functools.partial(norm_kernel, [pair[0].shape[1] for pair in gus], clip),
        grid_spec=pltpu.PrefetchScalarGridSpec(
            num_scalar_prefetch=1,
            grid=(blks,),
            in_specs=in_specs,
            out_specs=[pl.BlockSpec((ROWS, width), lambda j, *_: (j, 0)), whole(edge.shape)] + [whole(scale_t.shape)] * 2,
            scratch_shapes=[pltpu.VMEM(up_w.shape, BF16)] * 2
            + [pltpu.VMEM((width // LANES, ROWS, LANES), F32)]
            + [pltpu.VMEM((8, width), F32)] * 2,
        ),
        out_shape=[SDS((count // clips, width), F32), SDS(edge.shape, F32)] + [SDS(scale_t.shape, F32)] * 2,
        compiler_params=pltpu.CompilerParams(vmem_limit_bytes=VMEM),
        cost_estimate=pl.CostEstimate(flops=5_000_000_000, bytes_accessed=12_000_000, transcendentals=0),
        name="norm_grads",
    )(bands, *flat, up_w, after(waits, norm), istd, scale_t, *earlier)


def conv_kernel(
    clip, offsets, x_ref, x_up, x_down, edge_ref, gh_ref, gh_up, gh_down, gh_edge, gm_ref, conv_w, *refs
):
    o_gi, o_acc, pad4, gh4 = refs[-4:]
    blk, blks = pl.program_id(0), pl.num_programs(0)
    rows, width = x_ref.shape[1], x_ref.shape[2]
    tiles = width // LANES
    tm = lax.axis_index("tm")
    local = offsets[clip] - tm * blks * rows
    rows8 = edge_ref.shape[1]
    base = blk * rows

    @pl.when(blk == 0)
    def _():
        o_acc[...] = refs[0][...] if clip else jnp.zeros_like(o_acc)

    def masked(value, first):
        row = first + lax.broadcasted_iota(jnp.int32, value.shape, 0)
        return jnp.where(row >= local, value, 0.0)

    def above(edge, up):
        return jnp.where(blk == 0, jnp.where(tm > 0, edge[0], 0.0), up[0])

    def below(edge, down):
        return jnp.where(blk == blks - 1, jnp.where(tm > 0, 0.0, edge[0]), down[0])

    before, after = masked(above(edge_ref, x_up), base - rows8), masked(below(edge_ref, x_down), base + rows)
    g_before, g_after = above(gh_edge, gh_up), below(gh_edge, gh_down)
    middle = masked(x_ref[0], base)
    for t in range(tiles):
        lanes = slice(t * LANES, (t + 1) * LANES)
        pad4[t, 0:rows8, :] = before[:, lanes]
        pad4[t, rows8 : rows8 + rows, :] = middle[:, lanes]
        pad4[t, rows8 + rows :, :] = after[:, lanes]
        gh4[t, 0:rows8, :] = g_before[:, lanes]
        gh4[t, rows8 : rows8 + rows, :] = gh_ref[0, :, lanes]
        gh4[t, rows8 + rows :, :] = g_after[:, lanes]
    chunk = 64
    for r in range(0, rows, chunk):
        shown = base + r + lax.broadcasted_iota(jnp.int32, (chunk, LANES), 0) >= local
        for t in range(tiles):
            lanes = slice(t * LANES, (t + 1) * LANES)
            gh = gh4[t, rows8 + r : rows8 + r + chunk, :]
            o_acc[8 * KERNEL :, lanes] += fold8(gh)
            total = gm_ref[0, r : r + chunk, lanes]
            for k in range(KERNEL):
                first = r + rows8 + KERNEL // 2 - k
                total = total + conv_w[k : k + 1, lanes] * gh4[t, first : first + chunk, :]
                first = r + rows8 - KERNEL // 2 + k
                o_acc[8 * k : 8 * k + 8, lanes] += fold8(gh * pad4[t, first : first + chunk, :])
            o_gi[0, r : r + chunk, lanes] = jnp.where(shown, total, 0.0)


def run_conv(offsets, x, edge, gh, gh_edge, gm, conv_w, clip, so_far, waits=()):
    clips, frames, width = x.shape
    blks = frames // ROWS
    rows8 = edge.shape[1]
    mine = pl.BlockSpec((1, rows8, width), lambda j, *_: (clip, 0, 0))
    padded = pltpu.VMEM((width // LANES, ROWS + 2 * rows8, LANES), F32)
    blocks = row_halves(blks, ROWS, rows8, width, clip)
    in_specs = blocks + [mine] + row_halves(blks, ROWS, rows8, width, 0) + [mine] + blocks[:1]
    in_specs += [fixed(conv_w.shape)]
    operands = [x, x, x, edge, gh, gh, gh, gh_edge, after(waits, gm), conv_w]
    aliases = {}
    sums = (8 * (KERNEL + 1), width)
    if so_far:
        grads, acc = so_far
        operands.append(acc)
        in_specs.append(fixed(acc.shape))
        aliases = {1 + len(operands): 0}
        operands.append(grads)
        in_specs.append(pl.BlockSpec(memory_space=pl.ANY))
    return pl.pallas_call(
        functools.partial(conv_kernel, clip),
        grid_spec=pltpu.PrefetchScalarGridSpec(
            num_scalar_prefetch=1,
            grid=(blks,),
            in_specs=in_specs,
            out_specs=[blocks[0], whole(sums)],
            scratch_shapes=[padded, padded],
        ),
        out_shape=[SDS(x.shape, F32), SDS(sums, F32)],
        input_output_aliases=aliases,
        compiler_params=pltpu.CompilerParams(vmem_limit_bytes=VMEM),
        cost_estimate=pl.CostEstimate(flops=5_000_000_000, bytes_accessed=17_000_000, transcendentals=0),
        name="conv_grads",
    )(offsets, *operands)


def pack_kernel(acc, small, scales0, scales1, shifts0, shifts1, *refs):
    gubs, o_pack = refs[:-1], refs[-1]
    width = acc.shape[1]
    for k in range(KERNEL + 1):
        o_pack[k : k + 1, :] = jnp.sum(acc[8 * k : 8 * k + 8, :], axis=0, keepdims=True)
    o_pack[8:12, :] = scales0[...] + scales1[...]
    o_pack[12:16, :] = shifts0[...] + shifts1[...]
    o_pack[16:18, :] = small[1:3, :width]
    for i in range(3):
        o_pack[18 + i : 19 + i, :] = small[0:1, i * width : (i + 1) * width]
        gub = jnp.concatenate([v[...] for v in gubs], 1)
        o_pack[21 + i : 22 + i, :] = gub[:, i * width : (i + 1) * width]
    o_pack[24:, :] = jnp.zeros((o_pack.shape[0] - 24, width), F32)


def wave_kernel(
    first_blk, frames, scaled, offsets, spec, t1h, t1l, t2h, t2l, t0h, t0l, windows, inverse, *refs
):
    o_wave, o_tail, accs = refs[-3:]
    blk, clip = pl.program_id(0), pl.program_id(1)
    blks, clips = pl.num_programs(0), pl.num_programs(1)
    tiles = accs.shape[1]
    first = (first_blk + blk) * PAIRS
    local = offsets[clip] - lax.axis_index("tm") * frames
    acc5 = accs.at[clip]

    @pl.when(blk == 0)
    def _():
        for t in range(tiles):
            lanes = slice(t * LANES, (t + 1) * LANES)
            acc5[t, 0:8, :] = refs[0][0, :, lanes] if scaled else jnp.zeros((8, LANES), F32)

    @pl.when(blk > 0)
    def _():
        for t in range(tiles):
            acc5[t, 0:8, :] = acc5[t, PAIRS : PAIRS + 8, :]

    for t in range(tiles):
        acc5[t, 8:, :] = jnp.zeros((PAIRS, LANES), F32)

    n1, n2 = t1h.shape[0], t2h.shape[0]
    ab = dot3(split(spec[:, :n1]), (t1h[...], t1l[...]))
    cd = dot3(split(spec[:, n1 : n1 + n2]), (t2h[...], t2l[...]))
    p0 = dot3(split(spec[:, n1 + n2 :]), (t0h[...], t0l[...]))
    c1, c2, s1, s2 = fifths()
    sides = []
    for par in range(2):
        rows = slice(par * PAIRS, (par + 1) * PAIRS)
        w = p0.shape[1]
        a, b, c, d, p = ab[rows, :w], ab[rows, w:], cd[rows, :w], cd[rows, w:], p0[rows]
        e1, o1 = p + c1 * a + c2 * c, s1 * b + s2 * d
        e2, o2 = p + c2 * a + c1 * c, s2 * b - s1 * d
        v = [p + a + c, e1 - o1, e2 - o2, e2 + o2, e1 + o1]
        seg = []
        for t in range(2 * tiles):
            part = v[t // 2][:, (t % 2) * LANES : (t % 2 + 1) * LANES]
            seg.append(part * windows[par : par + 1, t * LANES : (t + 1) * LANES])
        sides.append(seg)
    even, odd = sides
    mid = tiles // 2
    right = lax.broadcasted_iota(jnp.int32, (PAIRS, LANES), 1) >= LANES // 2
    for t in range(tiles):
        here = even[t]
        if t > mid:
            here = here + odd[t]
        if t == mid:
            here = here + jnp.where(right, odd[t], 0.0)
        acc5[t, 0:PAIRS, :] += here
        acc5[t, 1 : PAIRS + 1, :] += even[tiles + t] + odd[tiles + t]
        if t < mid:
            acc5[t, 2 : PAIRS + 2, :] += odd[t]
        if t == mid:
            acc5[t, 2 : PAIRS + 2, :] += jnp.where(right, 0.0, odd[t])
        value = acc5[t, 0:PAIRS, :] * inverse_envelope(first, local, inverse, t, PAIRS)
        o_wave[pl.ds(clips * t + clip, PAIRS, stride=clips * tiles), :] = value

    @pl.when(blk == blks - 1)
    def _():
        for t in range(tiles):
            value = acc5[t, PAIRS : PAIRS + 8, :]
            if scaled:
                value = value * inverse_envelope(first + PAIRS, local, inverse, t, 8)
            o_tail[0, :, t * LANES : (t + 1) * LANES] = value


def run_wave(offsets, spec, consts, clips, first_blk, blks, earlier=(), waits=()):
    count, nfft = spec.shape
    all_blks = count // clips // ROWS
    tiles = nfft // 2 // LANES
    rows = clips * PAIRS * tiles
    in_specs = [pl.BlockSpec((ROWS, nfft), lambda j, i, *_: (i * all_blks + first_blk + j, 0))]
    in_specs += [fixed(v.shape) for v in consts]
    operands = [after(waits, spec), *consts]
    aliases = {}
    if earlier:
        carry, wave = earlier
        operands.append(carry)
        in_specs.append(pl.BlockSpec((1, 8, nfft // 2), lambda j, i, *_: (i, 0, 0)))
        aliases = {1 + len(operands): 0}
        operands.append(wave)
        in_specs.append(pl.BlockSpec(memory_space=pl.ANY))
    return pl.pallas_call(
        functools.partial(wave_kernel, first_blk, count // clips, first_blk == 0),
        grid_spec=pltpu.PrefetchScalarGridSpec(
            num_scalar_prefetch=1,
            grid=(blks, clips),
            in_specs=in_specs,
            out_specs=[
                pl.BlockSpec((rows, LANES), lambda j, i, *_: (first_blk + j, 0)),
                pl.BlockSpec((1, 8, nfft // 2), lambda j, i, *_: (i, 0, 0)),
            ],
            scratch_shapes=[pltpu.VMEM((clips, tiles, PAIRS + 8, LANES), F32)],
        ),
        out_shape=[SDS((rows * all_blks, LANES), F32), SDS((clips, 8, nfft // 2), F32)],
        input_output_aliases=aliases,
        compiler_params=pltpu.CompilerParams(vmem_limit_bytes=VMEM),
        cost_estimate=pl.CostEstimate(flops=5_000_000_000, bytes_accessed=8_000_000, transcendentals=0),
        name="wave",
    )(offsets, *operands)


def levels():
    clip = [("clip", 1 << i) for i in range((lax.axis_size("clip") - 1).bit_length())]
    tm = [("tm", 1 << i) for i in range((lax.axis_size("tm") - 1).bit_length())]
    return clip[:1] + clip[1:2] + tm + clip[2:]


def exchange(value, level):
    if level == "next":
        return lax.ppermute(value, "tm", [(i, i + 1) for i in range(lax.axis_size("tm") - 1)])
    across = {"clip": 0, "tm": 0}
    for axis, distance in level if isinstance(level, list) else [level]:
        across[axis] += distance
    if not across["tm"]:
        return lax.ppermute(value, "clip", [(i, i ^ across["clip"]) for i in range(lax.axis_size("clip"))])
    if not across["clip"]:
        return lax.ppermute(value, "tm", [(i, i ^ across["tm"]) for i in range(lax.axis_size("tm"))])
    n, m = lax.axis_size("clip"), lax.axis_size("tm")
    pairs = [(i * m + j, (i ^ across["clip"]) * m + (j ^ across["tm"])) for i in range(n) for j in range(m)]
    return lax.ppermute(value, ("clip", "tm"), pairs)


def side(level):
    axis, distance = level
    return lax.axis_index(axis) // distance % 2


class Sums:
    def __init__(self):
        self.running = []

    def add(self, steps, holds=()):
        entry = {"steps": steps, "holds": holds, "count": 0, "sent": None, "came": None, "left": 0, "sum": None}
        self.step(entry, None)
        self.running.append(entry)
        return entry

    def step(self, entry, values):
        try:
            entry["sent"] = entry["steps"].send(values)
            while entry["sent"][0][1] == levels()[0]:
                entry["sent"] = entry["steps"].send([exchange(*pair) for pair in entry["sent"]])
        except StopIteration as stop:
            entry["sent"], entry["sum"] = None, stop.value

    def waits(self):
        sent = []
        for entry in self.running:
            if entry["came"] is None and entry["sent"] is not None:
                entry["came"] = [exchange(*pair) for pair in entry["sent"]]
                entry["left"] = dict(entry["holds"]).get(entry["count"], 1)
                entry["count"] += 1
                sent += [pair[0] for pair in entry["sent"]]
        return sent

    def advance(self, results):
        done = []
        for entry in self.running:
            if entry["came"] is not None:
                entry["left"] -= 1
                if entry["left"] <= 0:
                    done.append(entry)
        if done:
            came, results = lax.optimization_barrier(([entry["came"] for entry in done], results))
            for entry, values in zip(done, came):
                entry["came"] = None
                self.step(entry, values)
        return results

    def finish(self, entry):
        while entry["sum"] is None:
            self.waits()
            self.advance(())
        return entry["sum"]


def halves_steps(keep, send, narrow):
    core, one, two, *last = levels()
    orders = ((one, two), (two, one))
    (came,) = yield [(send, core)]
    cols = keep.shape[1] // 2
    parts = [[(v, 0, c) for v in (keep, came)] for c in (0, cols)]

    def cut(terms, first):
        return [(v, row + first, col) for v, row, col in terms]

    def added(terms, rows):
        return sum(lax.dynamic_slice(v, (row, col), (rows, cols)) for v, row, col in terms)

    rows = keep.shape[0]
    for i in range(2):
        rows //= 2
        sides = [side(order[i]) for order in orders]
        came = yield [(added(cut(t, (1 - s) * rows), rows), o[i]) for t, s, o in zip(parts, sides, orders)]
        parts = [cut(t, s * rows) + [(c, 0, 0)] for t, s, c in zip(parts, sides, came)]
    value = jnp.concatenate([added(t, rows) for t in parts])
    halved = last if narrow and rows % (4 << len(last)) == 0 else []
    n, terms = value.shape[0], [(value, 0, 0)]
    for level in halved:
        n, s = n // 2, side(level)
        (came,) = yield [(added(cut(terms, (1 - s) * n), n), level)]
        terms = cut(terms, s * n) + [(came, 0, 0)]
    value = added(terms, n) if halved else value
    for level in last[len(halved) :]:
        (came,) = yield [(value, level)]
        value = value + came
    for level in halved[::-1]:
        s = side(level)
        (came,) = yield [(value, level)]
        value = jnp.concatenate([jnp.where(s == 0, value, came), jnp.where(s == 0, came, value)])
    parts = [value[:rows], value[rows:]]
    for i in (1, 0):
        came = yield [(part, order[i]) for part, order in zip(parts, orders)]
        parts = [jnp.concatenate(pair) for pair in zip(parts, came)]
    others = yield [(part, core) for part in parts]
    return parts, others, orders


def whole_steps(value):
    core, *rest = levels()
    (came,) = yield [(value, core)]
    value = value + came
    for pair in [rest[:1]] + [rest[i : i + 2] for i in range(1, len(rest), 2)]:
        came = yield [(value, [level]) for level in pair] + ([(value, pair)] if len(pair) == 2 else [])
        for other in came:
            value = value + other
    return value


def one_step(value, level):
    (came,) = yield [(value, level)]
    return came


def natural_blocks(orders, refs, copy):
    core = side(levels()[0])
    cols = refs[0].shape[1]
    rows = refs[0].shape[0] // 4
    for half in range(2):
        for here, pair in ((core == half, refs[:2]), (core != half, refs[2:])):

            @pl.when(here)
            def _(pair=pair, half=half):
                for i, (ref, order) in enumerate(zip(pair, orders)):
                    a, b = (side(level) for level in order)
                    for block in range(4):
                        first = (2 * jnp.bitwise_xor(block // 2, a) + jnp.bitwise_xor(block % 2, b)) * rows
                        value = ref[pl.ds(pl.multiple_of(first, 8), rows), :]
                        copy(half, slice(i * cols, (i + 1) * cols), block * rows, value)


def to_runs(runs):
    def copy(half, cols, first, value):
        for start, out, place, rows in runs:
            low, high = max(first, start), min(first + value.shape[0], start + rows)
            if low < high:
                at = place(half) + low - start
                out[at : at + high - low, cols] = value[low - first : high - first]

    return copy


def first_order_kernel(orders, *refs):
    o_head, o_down = refs[-2:]
    copy = to_runs(
        (
            (0, o_head, lambda half: half * (o_head.shape[0] // 2), o_head.shape[0] // 2),
            (HEAD_ROWS, o_down, lambda half: half * (o_down.shape[0] // 2), o_down.shape[0] // 2),
        )
    )
    natural_blocks(orders, refs[:4], copy)


def up_order_kernel(orders, *refs):
    o_up, up_t = refs[-2:]

    runs, at = [], 0
    for size, part in UP_PARTS:
        runs.append((at, up_t, lambda half, size=size, part=part: size * part + half * (size // 2), size // 2))
        at += size // 2
    copy = to_runs(runs)
    natural_blocks(orders, refs[:4], copy)
    for c in range(0, up_t.shape[0], LANES):
        o_up[:, c : c + LANES] = up_t[c : c + LANES, :].T


def run_order(kernel, total, out_shape, scratch=(), waits=()):
    parts, others, orders = total
    parts = after(waits, parts)
    return pl.pallas_call(
        functools.partial(kernel, orders),
        in_specs=[pl.BlockSpec(memory_space=pltpu.VMEM)] * 4,
        out_shape=out_shape,
        scratch_shapes=list(scratch),
        compiler_params=pltpu.CompilerParams(vmem_limit_bytes=VMEM),
        name="in_order",
    )(*parts, *others)


def unpack_kernel(pack, gcw, gcb, gscale, gshift, gls, gdb, ghb, gub):
    width = pack.shape[1]
    gcw[...] = pack[0:KERNEL, :]
    gcb[...] = pack[KERNEL : KERNEL + 1, :].reshape(width)
    gscale[...] = pack[8:12, :]
    gshift[...] = pack[12:16, :]
    gls[...] = pack[16:17, :].reshape(width)
    gdb[...] = pack[17:18, :].reshape(width)
    rows = [pack[18 + i : 19 + i, :] for i in range(6)]
    ghb[...] = jnp.concatenate(rows[:3], 1)[:, : ghb.shape[0]].reshape(ghb.shape[0])
    gub[...] = jnp.concatenate(rows[3:], 1).reshape(gub.shape[0])


def edges(value, index):
    n = value.shape[1]
    return jnp.where(index == 0, value[:, n - 8 :], value[:, :8])


def to_chunks(wave):
    clips, samples = wave.shape
    return wave.reshape(clips, samples // LANES, LANES).transpose(1, 0, 2).reshape(-1, LANES)


def from_chunks(chunks, clips):
    rows = chunks.shape[0] // clips
    return chunks.reshape(rows, clips, LANES).transpose(1, 0, 2).reshape(clips, rows * LANES)


def body(
    inputs,
    band_ids,
    offsets,
    conv_weight,
    conv_bias,
    scale_table,
    shift_table,
    up_weight,
    up_bias,
    down_weight,
    down_bias,
    layer_scale,
    head_weight,
    head_bias,
    wave_cotangent,
):
    clips, frames, width = inputs.shape
    assert lax.axis_size("tm") == 2
    nfft = head_weight.shape[1] - 2
    half = nfft // 2
    hidden = up_weight.shape[1]
    tm = lax.axis_index("tm")
    core = lax.axis_index("clip") % 2
    swap = lambda v: lax.ppermute(v, "tm", [(0, 1), (1, 0)])
    transforms, windows, inverse, turns = tables(nfft)
    dft = [jnp.asarray(v) for pair in transforms for v in pair]
    consts = dft + [jnp.asarray(windows), jnp.asarray(inverse)]

    edge = swap(edges(inputs, tm))
    cot_edge = swap(jnp.pad(wave_cotangent[:, :nfft].reshape(clips, 2, half), ((0, 0), (0, 6), (0, 0))))
    weights = (
        conv_weight,
        conv_bias,
        scale_table,
        shift_table,
        up_weight,
        up_bias,
        down_weight,
        down_bias,
        layer_scale,
        head_weight.T,
        head_bias,
    )
    (
        norm, istd, adt_h, adt_l, act_h, act_l, slope, spec, gm, gb_h, gb_l, gbt_h, gbt_l, hg_keep, hg_send, small,
    ) = run_head(
        band_ids, offsets, inputs, edge, to_chunks(wave_cotangent), cot_edge, weights, jnp.asarray(turns), consts
    )

    keep, send = run_down((gbt_h, gbt_l), (act_h, act_l), hg_keep, hg_send)
    sums = Sums()
    first_total = sums.add(halves_steps(keep, send, True))
    blks = frames // ROWS
    gus, gubs, halves = [], [], ()
    for size, part in UP_PARTS:
        results = run_up((gb_h, gb_l), slope, (adt_h, adt_l), down_weight, size, part, halves, waits=sums.waits())
        *halves, gub, gu_h, gu_l = sums.advance(results)
        gus.append((gu_h, gu_l))
        gubs.append(gub)
    up_total = sums.add(halves_steps(*halves, False), {3: 2})
    normed, gh_edge = [], edge
    for clip in range(clips):
        results = run_norm(band_ids, gus, up_weight, norm, istd, scale_table, gh_edge, clip, waits=sums.waits())
        gh_edge = results[1]
        normed.append(sums.advance(results))
    gh = [v[0][None] for v in normed]
    gh_edge = sums.add(one_step(normed[-1][1], ("tm", 1)))
    late = blks // 2
    wave, tail = run_wave(offsets, spec, consts, clips, late, blks - late, waits=sums.waits())
    wave, tail = sums.advance((wave, tail))
    arrived = sums.add(one_step(tail, "next"))
    gh_edge = sums.finish(gh_edge)
    so_far = ()
    gm = gm.reshape(clips, frames, width)
    for clip in range(clips):
        so_far = run_conv(
            offsets, inputs, edge, gh[clip], gh_edge, gm, conv_weight, clip, so_far, waits=sums.waits()
        )
        so_far = sums.advance(so_far)
    grad_inputs, acc = so_far
    pack = pl.pallas_call(pack_kernel, out_shape=SDS((32, width), F32), name="pack")(
        acc, small, *[v[2] for v in normed], *[v[3] for v in normed], *gubs
    )
    small_total = sums.add(whole_steps(pack))

    arrived = sums.finish(arrived)
    wave, over = run_wave(offsets, spec, consts, clips, 0, late, (arrived, wave), waits=sums.waits())
    wave, over = sums.advance((wave, over))
    over = to_chunks(over[:, :2].reshape(clips, nfft))
    at = late * clips * PAIRS * half // LANES
    mended = lax.dynamic_slice_in_dim(wave, at, over.shape[0]) + over
    waveform = from_chunks(lax.dynamic_update_slice_in_dim(wave, mended, at, 0), clips)

    first_total = sums.finish(first_total)
    head_grad, down_grad = sums.advance(
        run_order(
            first_order_kernel,
            first_total,
            [SDS((nfft + 2, width), F32), SDS((hidden, width), F32)],
            waits=sums.waits(),
        )
    )
    up_total = sums.finish(up_total)
    (up_grad,) = sums.advance(
        run_order(
            up_order_kernel,
            up_total,
            [SDS((width, hidden), F32)],
            [pltpu.VMEM((hidden, width), F32)],
            waits=sums.waits(),
        )
    )
    pack = sums.finish(small_total)
    small_shapes = [(KERNEL, width), (width,), scale_table.shape, scale_table.shape]
    small_shapes += [(width,), (width,), (nfft + 2,), (hidden,)]
    gcw, gcb, gscale, gshift, gls, gdb, ghb, gub = pl.pallas_call(
        unpack_kernel, out_shape=[SDS(shape, F32) for shape in small_shapes], name="unpack"
    )(pack)
    return (
        waveform,
        grad_inputs,
        gcw,
        gcb,
        gscale,
        gshift,
        up_grad,
        gub,
        down_grad,
        gdb,
        gls,
        head_grad.T,
        ghb,
    )


def solution(mesh):
    in_specs = (P("clip", "tm", None), P("clip"), P("clip")) + (P(),) * 11 + (P("clip", "tm"),)
    out_specs = (P("clip", "tm"), P("clip", "tm", None)) + (P(),) * 11
    return jax.shard_map(body, mesh=mesh, in_specs=in_specs, out_specs=out_specs, check_vma=False)
```

profile of v0, /device:TPU:0, one launch (start us, length us, event | category | flops | bytes accessed | tf_op | source)
XLA Modules:
  0.0 292.6 jit_solution(3771949807364832714)
XLA Ops:
  1.4 3.0 %collective-permute-start.1 = (f32[2,8,640]{2,1,0:T(8,128)S(1)}, f32[2,8,640]{2,1,0:T(8,128)S(1)}, u32[]{:S(2)}, u32[]{:S(2)}) collective-permute-start(f32[2,8,640]{2,1,0:T(8,128)S(1)} %pad.4), channel_id=1, source_target_pairs={{0,1},{1,0},{2,3},{3,2},{4,5},{5,4},{6,7},{7,6},{8,9},{9,8},{10,11... | collective-permute-start | bytes 122888 | tf_op jit(solution)/shard_map/ppermute | solution.py:1200
  5.2 3.9 %collective-permute-done.edge_ref = f32[2,8,512]{2,1,0:T(8,128)S(1)} collective-permute-done((f32[2,8,512]{2,1,0:T(8,128)S(1)}, f32[2,8,512]{2,1,0:T(8,128)S(1)}, u32[]{:S(2)}, u32[]{:S(2)}) %collective-permute-start) | collective-permute-done | bytes 32800 | tf_op jit(solution)/shard_map/ppermute | solution.py:1200
  9.7 85.7 %head.1 = (f32[2048,512]{1,0:T(8,128)}, f32[2048,128]{1,0:T(8,128)}, bf16[512,2048]{1,0:T(8,128)(2,1)}, bf16[512,2048]{1,0:T(8,128)(2,1)}, bf16[2048,1536]{1,0:T...) custom-call(s32[2]{0:T(128)} %bands.5, s32[2]{0:T(128)} %offsets.9, ...), custom_call_target="tpu_custom_call" | custom-call | flops 80000000000 | bytes 90000000 | tf_op jit(solution)/shard_map/head/pallas_call | solution.py:534
  95.4 15.4 %down_grads.1 = (f32[1472,512]{1,0:T(8,128)}, f32[1472,512]{1,0:T(8,128)}) custom-call(bf16[512,2048]{1,0:T(8,128)(2,1)} %get-tuple-element.136.gbt_h, bf16[512,2048]{1,0:T(8,128)(2,1)} %get-tuple-element.137.gbt_l, bf16[2048,1536]{1,0:T(8,128)(2,1)} %get-tuple-element.138.act_h, ...), custom_call_target="tpu_custom_call", output_to_operand_aliasing={{0}: (4, {}), {1}: (5, {})} | custom-call | flops 10000000000 | bytes 20000000 | tf_op jit(solution)/shard_map/down_grads/pallas_call | solution.py:581
  111.0 5.6 %collective-permute-done.2 = f32[1472,512]{1,0:T(8,128)S(1)} collective-permute-done((f32[1472,512]{1,0:T(8,128)}, f32[1472,512]{1,0:T(8,128)S(1)}, u32[]{:S(2)}, u32[]{:S(2)}) %collective-permute-start.2) | collective-permute-done | bytes 3014688 | tf_op jit(solution)/shard_map/ppermute | solution.py:963
  116.5 2.7 dynamic-slice_add_fusion
  119.2 1.5 collective-permute-start.3
  121.2 21.1 %up_grads.2 = (f32[768,512]{1,0:T(8,128)}, f32[768,512]{1,0:T(8,128)}, f32[1,1024]{1,0:T(1,128)}, bf16[2048,1024]{1,0:T(8,128)(2,1)}, bf16[2048,1024]{1,0:T(8,128)(2,1)}) custom-call(bf16[2048,512]{1,0:T(8,128)(2,1)} %get-tuple-element.144.gb_h, bf16[2048,512]{1,0:T(8,128)(2,1)} %get-tuple-element.145.gb_l, f32[2048,1536]{1,0:T(8,128)} %get-tuple-element.157.slope, ...), custom_call_target="tpu_custom_call" | custom-call | flops 10000000000 | bytes 20000000 | tf_op jit(solution)/shard_map/up_grads/pallas_call | solution.py:639
  142.3 2.5 dynamic-slice_add_fusion.4
  144.8 1.5 collective-permute-start.5
  146.9 12.5 %up_grads.3 = (f32[768,512]{1,0:T(8,128)}, f32[768,512]{1,0:T(8,128)}, f32[1,512]{1,0:T(1,128)}, bf16[2048,512]{1,0:T(8,128)(2,1)}, bf16[2048,512]{1,0:T(8,128)(2,1)}) custom-call(bf16[2048,512]{1,0:T(8,128)(2,1)} %get-tuple-element.144.gb_h, bf16[2048,512]{1,0:T(8,128)(2,1)} %get-tuple-element.145.gb_l, ...), custom_call_target="tpu_custom_call", output_to_operand_aliasing={{0}: (6, {}), {1}: (7, {})} | custom-call | flops 10000000000 | bytes 20000000 | tf_op jit(solution)/shard_map/up_grads/pallas_call | solution.py:639
  159.7 1.9 add_add_fusion
  162.5 1.6 collective-permute-start.7
  164.1 2.0 dynamic-slice_add_fusion.2
  166.5 1.5 collective-permute-start.9
  168.0 11.6 %norm_grads.2 = (f32[1024,512]{1,0:T(8,128)}, f32[2,8,512]{2,1,0:T(8,128)}, f32[4,512]{1,0:T(4,128)}, f32[4,512]{1,0:T(4,128)}) custom-call(s32[2]{0:T(128)} %bands.5, bf16[2048,1024]{1,0:T(8,128)(2,1)} %get-tuple-element.169.refs_0_, bf16[2048,1024]{1,0:T(8,128)(2,1)} %get-tuple-element.170.refs_1_, bf16[2048,512]{1,0:T(8,128)(2,1)} %get-tuple-element.171.refs_2_, ...), custom_call_target="tpu_custom_call" | custom-call | flops 5000000000 | bytes 12000000 | tf_op jit(solution)/shard_map/norm_grads/pallas_call | solution.py:722
  179.7 1.1 dynamic-slice_add_fusion.6
  180.8 1.6 collective-permute-start.12
  182.9 1.7 fusion.2
  184.6 2.6 collective-permute-start.11
  187.1 11.7 %norm_grads.3 = (f32[1024,512]{1,0:T(8,128)}, f32[2,8,512]{2,1,0:T(8,128)}, f32[4,512]{1,0:T(4,128)}, f32[4,512]{1,0:T(4,128)}) custom-call(s32[2]{0:T(128)} %bands.5, bf16[2048,1024]{1,0:T(8,128)(2,1)} %get-tuple-element.169.refs_0_, bf16[2048,1024]{1,0:T(8,128)(2,1)} %get-tuple-element.170.refs_1_, bf16[2048,512]{1,0:T(8,128)(2,1)} %get-tuple-element.171.refs_2_, ...), custom_call_target="tpu_custom_call" | custom-call | flops 5000000000 | bytes 12000000 | tf_op jit(solution)/shard_map/norm_grads/pallas_call | solution.py:722
  198.9 1.1 add_add_fusion.3
  200.9 1.1 fusion.5
  202.9 9.8 %wave.2 = (f32[5120,128]{1,0:T(8,128)}, f32[2,8,640]{2,1,0:T(8,128)}) custom-call(s32[2]{0:T(128)} %offsets.9, f32[2048,1280]{1,0:T(8,128)} %get-tuple-element.223.spec, bf16[512,512]{1,0:T(8,128)(2,1)} %constant.144.clone.t1h, bf16[512,512]{1,0:T(8,128)(2,1)} %constant.145.clone.t1l, bf16[512,512]{1,0:T(8,128)(2,1)} %constant.146.clone.t2h, ...), custom_call_target="tpu_custom_call" | custom-call | flops 5000000000 | bytes 8000000 | tf_op jit(solution)/shard_map/wave/pallas_call | solution.py:930
  214.3 3.3 %collective-permute-start.18 = (f32[2,8,640]{2,1,0:T(8,128)S(1)}, f32[2,8,640]{2,1,0:T(8,128)S(1)}, u32[]{:S(2)}, u32[]{:S(2)}) collective-permute-start(f32[2,8,640]{2,1,0:T(8,128)S(1)} %copy-done.13), channel_id=1, source_target_pairs={{0,1},{2,3},{4,5},{6,7},{8,9},{10,11},{12,13},{14,15},{16,17},{18,... | collective-permute-start | bytes 122888 | tf_op jit(solution)/shard_map/ppermute | solution.py:958
  217.6 2.6 collective-permute-start.21
  220.3 6.7 %conv_grads.2 = (f32[2,1024,512]{2,1,0:T(8,128)}, f32[64,512]{1,0:T(8,128)}) custom-call(s32[2]{0:T(128)} %offsets.9, f32[2,1024,512]{2,1,0:T(8,128)} %x_down.5, f32[2,1024,512]{2,1,0:T(8,128)} %x_down.5, f32[2,1024,512]{2,1,0:T(8,128)} %x_down.5, f32[2,8,512]{2,1,0:T(8,128)} %copy-done.10, f32[1,1024,512]{2,1,0:T(8,128)} %bitcast.16, ...), custom_call_target="tpu_custom_call" | custom-call | flops 5000000000 | bytes 17000000 | tf_op jit(solution)/shard_map/conv_grads/pallas_call | solution.py:812
  227.6 2.6 collective-permute-start.19
  230.2 1.5 collective-permute-start.20
  231.7 7.1 %conv_grads.3 = (f32[2,1024,512]{2,1,0:T(8,128)}, f32[64,512]{1,0:T(8,128)}) custom-call(s32[2]{0:T(128)} %offsets.9, f32[2,1024,512]{2,1,0:T(8,128)} %x_down.5, f32[2,1024,512]{2,1,0:T(8,128)} %x_down.5, f32[2,1024,512]{2,1,0:T(8,128)} %x_down.5, f32[2,8,512]{2,1,0:T(8,128)} %copy-done.10, ...), custom_call_target="tpu_custom_call", output_to_operand_aliasing={{0}: (12, {})} | custom-call | flops 5000000000 | bytes 17000000 | tf_op jit(solution)/shard_map/conv_grads/pallas_call | solution.py:812
  241.4 1.6 pack.1
  243.1 2.1 collective-permute-start.24
  245.2 1.3 collective-permute-start.25
  248.2 9.9 %wave.3 = (f32[5120,128]{1,0:T(8,128)}, f32[2,8,640]{2,1,0:T(8,128)}) custom-call(s32[2]{0:T(128)} %offsets.9, f32[2048,1280]{1,0:T(8,128)} %get-tuple-element.223.spec, bf16[512,512]{1,0:T(8,128)(2,1)} %constant.144.clone.t1h, bf16[512,512]{1,0:T(8,128)(2,1)} %constant.145.clone.t1l, ...), custom_call_target="tpu_custom_call", output_to_operand_aliasing={{0}: (11, {})} | custom-call | flops 5000000000 | bytes 8000000 | tf_op jit(solution)/shard_map/wave/pallas_call | solution.py:930
  258.0 2.3 collective-permute-done.27
  260.3 1.2 pad_maximum_fusion.1.refs_1_
  261.7 1.7 pad_maximum_fusion.refs_0_
  263.5 1.7 collective-permute-start.29
  267.6 1.1 copy-done.7
  268.8 1.7 collective-permute-start.32
  270.5 5.8 %in_order.2 = (f32[1282,512]{1,0:T(8,128)}, f32[1536,512]{1,0:T(8,128)}) custom-call(f32[1472,256]{1,0:T(8,128)} %copy-done.1, f32[1472,256]{1,0:T(8,128)} %copy-done, f32[1472,256]{1,0:T(8,128)} %copy-done.7, f32[1472,256]{1,0:T(8,128)} %copy-done.6), custom_call_target="tpu_custom_call" | custom-call | tf_op jit(solution)/shard_map/in_order/pallas_call | solution.py:1138
  276.2 1.7 collective-permute-done.30
  277.9 1.0 pad_maximum_fusion.3.refs_1_
  279.1 1.3 pad_maximum_fusion.2.refs_0_
  281.5 1.4 collective-permute-start.35
  283.6 1.3 dynamic_update_slice.3
  285.8 4.6 %in_order.3 = f32[512,1536]{1,0:T(8,128)} custom-call(f32[768,256]{1,0:T(8,128)} %copy-done.3, f32[768,256]{1,0:T(8,128)} %copy-done.2, f32[768,256]{1,0:T(8,128)} %collective-permute-done.36.refs_2_, f32[768,256]{1,0:T(8,128)} %copy-done.8), custom_call_target="tpu_custom_call" | custom-call | tf_op jit(solution)/shard_map/in_order/pallas_call | solution.py:1138
  291.1 1.5 unpack.1
  (112 shorter events, 19.6 us)
Async XLA Ops:
  1.4 7.7 %collective-permute-start.1 = (f32[2,8,640]{2,1,0:T(8,128)S(1)}, f32[2,8,640]{2,1,0:T(8,128)S(1)}, u32[]{:S(2)}, u32[]{:S(2)}) collective-permute-start(f32[2,8,640]{2,1,0:T(8,128)S(1)} %pad.4), channel_id=1, source_target_pairs={{0,1},{1,0},{2,3},{3,2},{4,5},{5,4},{6,7},{7,6},{8,9},{9,8},{10,11... | collective-permute-start | bytes 122888 | tf_op jit(solution)/shard_map/ppermute | solution.py:1200
  5.2 3.9 %collective-permute-start = (f32[2,8,512]{2,1,0:T(8,128)S(1)}, f32[2,8,512]{2,1,0:T(8,128)S(1)}, u32[]{:S(2)}, u32[]{:S(2)}) collective-permute-start(f32[2,8,512]{2,1,0:T(8,128)S(1)} %slice_select_fusion), channel_id=1, source_target_pairs={{0,1},{1,0},{2,3},{3,2},{4,5},{5,4},{6,7},{7,6},{8,9},{9,8},{10,11... | collective-permute-start | bytes 98312 | tf_op jit(solution)/shard_map/ppermute | solution.py:1200
  110.8 5.7 %collective-permute-start.2 = (f32[1472,512]{1,0:T(8,128)}, f32[1472,512]{1,0:T(8,128)S(1)}, u32[]{:S(2)}, u32[]{:S(2)}) collective-permute-start(f32[1472,512]{1,0:T(8,128)} %get-tuple-element.143), channel_id=1, source_target_pairs={{0,2},{2,0},{4,6},{6,4},{8,10},{10,8},{12,14},{14,12},{16,18},{18,... | collective-permute-start | bytes 9043976 | tf_op jit(solution)/shard_map/ppermute | solution.py:963
  119.2 23.1 %collective-permute-start.3 = (f32[736,256]{1,0:T(8,128)}, f32[736,256]{1,0:T(8,128)S(1)}, u32[]{:S(2)}, u32[]{:S(2)}) collective-permute-start(f32[736,256]{1,0:T(8,128)} %get-tuple-element.264), channel_id=1, source_target_pairs={{0,4},{2,6},{4,0},{6,2},{8,12},{10,14},{12,8},{14,10},{16,20},{18,... | collective-permute-start | bytes 2261000 | tf_op jit(solution)/shard_map/ppermute | solution.py:963
  120.7 21.6 %collective-permute-start.4 = (f32[736,256]{1,0:T(8,128)}, f32[736,256]{1,0:T(8,128)}, u32[]{:S(2)}, u32[]{:S(2)}) collective-permute-start(f32[736,256]{1,0:T(8,128)} %get-tuple-element.263), channel_id=1, source_target_pairs={{0,1},{1,0},{2,3},{3,2},{4,5},{5,4},{6,7},{7,6},{8,9},{9,8},{10,11... | collective-permute-start | bytes 2261000 | tf_op jit(solution)/shard_map/ppermute | solution.py:965
  142.3 17.1 %copy-start.9 = (f32[736,256]{1,0:T(8,128)}, f32[736,256]{1,0:T(8,128)S(1)}, u32[]{:S(2)}) copy-start(f32[736,256]{1,0:T(8,128)S(1)} %collective-permute-done.3) | copy-start | bytes 2260996
  144.8 14.6 %collective-permute-start.5 = (f32[368,256]{1,0:T(8,128)}, f32[368,256]{1,0:T(8,128)}, u32[]{:S(2)}, u32[]{:S(2)}) collective-permute-start(f32[368,256]{1,0:T(8,128)} %get-tuple-element.262), channel_id=1, source_target_pairs={{0,1},{1,0},{2,3},{3,2},{4,5},{5,4},{6,7},{7,6},{8,9},{9,8},{10,11... | collective-permute-start | bytes 1130504 | tf_op jit(solution)/shard_map/ppermute | solution.py:965
  146.4 13.1 %collective-permute-start.6 = (f32[368,256]{1,0:T(8,128)}, f32[368,256]{1,0:T(8,128)}, u32[]{:S(2)}, u32[]{:S(2)}) collective-permute-start(f32[368,256]{1,0:T(8,128)} %get-tuple-element.261), channel_id=1, source_target_pairs={{0,4},{2,6},{4,0},{6,2},{8,12},{10,14},{12,8},{14,10},{16,20},{18,... | collective-permute-start | bytes 1130504 | tf_op jit(solution)/shard_map/ppermute | solution.py:963
  159.5 4.6 %collective-permute-start.8 = (f32[768,512]{1,0:T(8,128)}, f32[768,512]{1,0:T(8,128)}, u32[]{:S(2)}, u32[]{:S(2)}) collective-permute-start(f32[768,512]{1,0:T(8,128)} %get-tuple-element.168), channel_id=1, source_target_pairs={{0,2},{2,0},{4,6},{6,4},{8,10},{10,8},{12,14},{14,12},{16,18},{18,... | collective-permute-start | bytes 4718600 | tf_op jit(solution)/shard_map/ppermute | solution.py:963
  159.7 4.3 %copy-start.4 = (f32[768,512]{1,0:T(8,128)S(1)}, f32[768,512]{1,0:T(8,128)}, u32[]{:S(2)}) copy-start(f32[768,512]{1,0:T(8,128)} %get-tuple-element.167) | copy-start | bytes 4718596
  162.5 17.1 %collective-permute-start.7 = (f32[368,256]{1,0:T(8,128)}, f32[368,256]{1,0:T(8,128)}, u32[]{:S(2)}, u32[]{:S(2)}) collective-permute-start(f32[368,256]{1,0:T(8,128)} %fusion), channel_id=1, source_target_pairs={{0,8},{2,10},{4,12},{6,14},{8,0},{10,2},{12,4},{14,6},{16,24},{18,... | collective-permute-start | bytes 1130504 | tf_op jit(solution)/shard_map/ppermute | solution.py:963
  166.0 13.6 %collective-permute-start.10 = (f32[384,256]{1,0:T(8,128)}, f32[384,256]{1,0:T(8,128)S(1)}, u32[]{:S(2)}, u32[]{:S(2)}) collective-permute-start(f32[384,256]{1,0:T(8,128)} %get-tuple-element.269), channel_id=1, source_target_pairs={{0,1},{1,0},{2,3},{3,2},{4,5},{5,4},{6,7},{7,6},{8,9},{9,8},{10,11... | collective-permute-start | bytes 1179656 | tf_op jit(solution)/shard_map/ppermute | solution.py:965
  166.5 13.1 %collective-permute-start.9 = (f32[384,256]{1,0:T(8,128)S(1)}, f32[384,256]{1,0:T(8,128)S(1)}, u32[]{:S(2)}, u32[]{:S(2)}) collective-permute-start(f32[384,256]{1,0:T(8,128)S(1)} %get-tuple-element.270), channel_id=1, source_target_pairs={{0,4},{2,6},{4,0},{6,2},{8,12},{10,14},{12,8},{14,10},{16,20},{18,... | collective-permute-start | bytes 1179656 | tf_op jit(solution)/shard_map/ppermute | solution.py:963
  168.0 11.6 %copy-start.5 = (f32[768,512]{1,0:T(8,128)S(1)}, f32[768,512]{1,0:T(8,128)}, u32[]{:S(2)}) copy-start(f32[768,512]{1,0:T(8,128)} %get-tuple-element.167) | copy-start | bytes 4718596
  180.8 18.1 %collective-permute-start.12 = (f32[192,256]{1,0:T(8,128)S(1)}, f32[192,256]{1,0:T(8,128)S(1)}, u32[]{:S(2)}, u32[]{:S(2)}) collective-permute-start(f32[192,256]{1,0:T(8,128)S(1)} %get-tuple-element.268), channel_id=1, source_target_pairs={{0,1},{1,0},{2,3},{3,2},{4,5},{5,4},{6,7},{7,6},{8,9},{9,8},{10,11... | collective-permute-start | bytes 589832 | tf_op jit(solution)/shard_map/ppermute | solution.py:965
  182.4 16.5 %collective-permute-start.13 = (f32[192,256]{1,0:T(8,128)S(1)}, f32[192,256]{1,0:T(8,128)S(1)}, u32[]{:S(2)}, u32[]{:S(2)}) collective-permute-start(f32[192,256]{1,0:T(8,128)S(1)} %get-tuple-element.267), channel_id=1, source_target_pairs={{0,4},{2,6},{4,0},{6,2},{8,12},{10,14},{12,8},{14,10},{16,20},{18,... | collective-permute-start | bytes 589832 | tf_op jit(solution)/shard_map/ppermute | solution.py:963
  184.6 14.3 %collective-permute-start.11 = (f32[184,256]{1,0:T(8,128)}, f32[184,256]{1,0:T(8,128)}, u32[]{:S(2)}, u32[]{:S(2)}) collective-permute-start(f32[184,256]{1,0:T(8,128)} %fusion.2), channel_id=1, source_target_pairs={{0,16},{2,18},{4,20},{6,22},{8,24},{10,26},{12,28},{14,30},{16,0},... | collective-permute-start | bytes 565256 | tf_op jit(solution)/shard_map/ppermute | solution.py:963
  198.9 3.6 %copy-start.15 = (f32[2,8,512]{2,1,0:T(8,128)S(1)}, f32[2,8,512]{2,1,0:T(8,128)}, u32[]{:S(2)}) copy-start(f32[2,8,512]{2,1,0:T(8,128)} %get-tuple-element.191) | copy-start | bytes 98308
  200.1 13.7 %collective-permute-start.15 = (f32[384,256]{1,0:T(8,128)S(1)}, f32[384,256]{1,0:T(8,128)S(1)}, u32[]{:S(2)}, u32[]{:S(2)}) collective-permute-start(f32[384,256]{1,0:T(8,128)S(1)} %pad_maximum_fusion.6), channel_id=1, source_target_pairs={{0,8},{2,10},{4,12},{6,14},{8,0},{10,2},{12,4},{14,6},{16,24},{18,... | collective-permute-start | bytes 1179656 | tf_op jit(solution)/shard_map/ppermute | solution.py:963
  202.0 10.8 %collective-permute-start.14 = (f32[184,256]{1,0:T(8,128)S(1)}, f32[184,256]{1,0:T(8,128)S(1)}, u32[]{:S(2)}, u32[]{:S(2)}) collective-permute-start(f32[184,256]{1,0:T(8,128)S(1)} %fusion.5), channel_id=1, source_target_pairs={{0,16},{2,18},{4,20},{6,22},{8,24},{10,26},{12,28},{14,30},{16,0},... | collective-permute-start | bytes 565256 | tf_op jit(solution)/shard_map/ppermute | solution.py:963
  202.4 10.3 %collective-permute-start.16 = (f32[2,8,512]{2,1,0:T(8,128)S(1)}, f32[2,8,512]{2,1,0:T(8,128)S(1)}, u32[]{:S(2)}, u32[]{:S(2)}) collective-permute-start(f32[2,8,512]{2,1,0:T(8,128)S(1)} %copy-done.15), channel_id=1, source_target_pairs={{0,1},{1,0},{2,3},{3,2},{4,5},{5,4},{6,7},{7,6},{8,9},{9,8},{10,11... | collective-permute-start | bytes 98312 | tf_op jit(solution)/shard_map/ppermute | solution.py:965
  212.7 7.5 %copy-start.11 = (f32[2,8,512]{2,1,0:T(8,128)}, f32[2,8,512]{2,1,0:T(8,128)S(1)}, u32[]{:S(2)}) copy-start(f32[2,8,512]{2,1,0:T(8,128)S(1)} %collective-permute-done.16.gh_edge) | copy-start | bytes 98308
  213.9 13.6 %collective-permute-start.17 = (f32[368,256]{1,0:T(8,128)S(1)}, f32[368,256]{1,0:T(8,128)S(1)}, u32[]{:S(2)}, u32[]{:S(2)}) collective-permute-start(f32[368,256]{1,0:T(8,128)S(1)} %pad_maximum_fusion.9), channel_id=1, source_target_pairs={{0,8},{2,10},{4,12},{6,14},{8,0},{10,2},{12,4},{14,6},{16,24},{18,... | collective-permute-start | bytes 1130504 | tf_op jit(solution)/shard_map/ppermute | solution.py:963
  214.3 12.7 %collective-permute-start.18 = (f32[2,8,640]{2,1,0:T(8,128)S(1)}, f32[2,8,640]{2,1,0:T(8,128)S(1)}, u32[]{:S(2)}, u32[]{:S(2)}) collective-permute-start(f32[2,8,640]{2,1,0:T(8,128)S(1)} %copy-done.13), channel_id=1, source_target_pairs={{0,1},{2,3},{4,5},{6,7},{8,9},{10,11},{12,13},{14,15},{16,17},{18,... | collective-permute-start | bytes 122888 | tf_op jit(solution)/shard_map/ppermute | solution.py:958
  217.6 21.2 %collective-permute-start.21 = (f32[384,256]{1,0:T(8,128)S(1)}, f32[384,256]{1,0:T(8,128)S(1)}, u32[]{:S(2)}, u32[]{:S(2)}) collective-permute-start(f32[384,256]{1,0:T(8,128)S(1)} %fusion.6), channel_id=1, source_target_pairs={{0,16},{2,18},{4,20},{6,22},{8,24},{10,26},{12,28},{14,30},{16,0},... | collective-permute-start | bytes 1179656 | tf_op jit(solution)/shard_map/ppermute | solution.py:963
  227.0 11.8 %copy-start.12 = (f32[2,8,640]{2,1,0:T(8,128)}, f32[2,8,640]{2,1,0:T(8,128)S(1)}, u32[]{:S(2)}) copy-start(f32[2,8,640]{2,1,0:T(8,128)S(1)} %collective-permute-done.18.refs_0_) | copy-start | bytes 122884
  227.6 11.2 %collective-permute-start.19 = (f32[368,256]{1,0:T(8,128)S(1)}, f32[368,256]{1,0:T(8,128)S(1)}, u32[]{:S(2)}, u32[]{:S(2)}) collective-permute-start(f32[368,256]{1,0:T(8,128)S(1)} %get-tuple-element.272), channel_id=1, source_target_pairs={{0,1},{1,0},{2,3},{3,2},{4,5},{5,4},{6,7},{7,6},{8,9},{9,8},{10,11... | collective-permute-start | bytes 1130504 | tf_op jit(solution)/shard_map/ppermute | solution.py:965
  230.2 8.6 %collective-permute-start.20 = (f32[368,256]{1,0:T(8,128)S(1)}, f32[368,256]{1,0:T(8,128)S(1)}, u32[]{:S(2)}, u32[]{:S(2)}) collective-permute-start(f32[368,256]{1,0:T(8,128)S(1)} %get-tuple-element.271), channel_id=1, source_target_pairs={{0,4},{2,6},{4,0},{6,2},{8,12},{10,14},{12,8},{14,10},{16,20},{18,... | collective-permute-start | bytes 1130504 | tf_op jit(solution)/shard_map/ppermute | solution.py:963
  240.7 19.7 %collective-permute-start.23 = (f32[736,256]{1,0:T(8,128)}, f32[736,256]{1,0:T(8,128)}, u32[]{:S(2)}, u32[]{:S(2)}) collective-permute-start(f32[736,256]{1,0:T(8,128)} %pad_maximum_fusion.5), channel_id=1, source_target_pairs={{0,1},{1,0},{2,3},{3,2},{4,5},{5,4},{6,7},{7,6},{8,9},{9,8},{10,11... | collective-permute-start | bytes 2261000 | tf_op jit(solution)/shard_map/ppermute | solution.py:965
  240.7 19.6 %collective-permute-start.22 = (f32[736,256]{1,0:T(8,128)}, f32[736,256]{1,0:T(8,128)}, u32[]{:S(2)}, u32[]{:S(2)}) collective-permute-start(f32[736,256]{1,0:T(8,128)} %pad_maximum_fusion.4), channel_id=1, source_target_pairs={{0,4},{2,6},{4,0},{6,2},{8,12},{10,14},{12,8},{14,10},{16,20},{18,... | collective-permute-start | bytes 2261000 | tf_op jit(solution)/shard_map/ppermute | solution.py:963
  243.0 3.5 %collective-permute-start.26 = (f32[32,512]{1,0:T(8,128)}, f32[32,512]{1,0:T(8,128)S(1)}, u32[]{:S(2)}, u32[]{:S(2)}) collective-permute-start(f32[32,512]{1,0:T(8,128)} %pack.1), channel_id=1, source_target_pairs={{0,2},{2,0},{4,6},{6,4},{8,10},{10,8},{12,14},{14,12},{16,18},{18,... | collective-permute-start | bytes 196616 | tf_op jit(solution)/shard_map/ppermute | solution.py:963
  243.1 17.2 %collective-permute-start.24 = (f32[192,256]{1,0:T(8,128)S(1)}, f32[192,256]{1,0:T(8,128)S(1)}, u32[]{:S(2)}, u32[]{:S(2)}) collective-permute-start(f32[192,256]{1,0:T(8,128)S(1)} %get-tuple-element.274), channel_id=1, source_target_pairs={{0,1},{1,0},{2,3},{3,2},{4,5},{5,4},{6,7},{7,6},{8,9},{9,8},{10,11... | collective-permute-start | bytes 589832 | tf_op jit(solution)/shard_map/ppermute | solution.py:965
  245.2 15.1 %collective-permute-start.25 = (f32[192,256]{1,0:T(8,128)S(1)}, f32[192,256]{1,0:T(8,128)S(1)}, u32[]{:S(2)}, u32[]{:S(2)}) collective-permute-start(f32[192,256]{1,0:T(8,128)S(1)} %get-tuple-element.273), channel_id=1, source_target_pairs={{0,4},{2,6},{4,0},{6,2},{8,12},{10,14},{12,8},{14,10},{16,20},{18,... | collective-permute-start | bytes 589832 | tf_op jit(solution)/shard_map/ppermute | solution.py:963
  247.4 12.9 %collective-permute-start.27 = (f32[32,512]{1,0:T(8,128)S(1)}, f32[32,512]{1,0:T(8,128)S(1)}, u32[]{:S(2)}, u32[]{:S(2)}) collective-permute-start(f32[32,512]{1,0:T(8,128)S(1)} %add.328), channel_id=1, source_target_pairs={{0,4},{2,6},{4,0},{6,2},{8,12},{10,14},{12,8},{14,10},{16,20},{18,... | collective-permute-start | bytes 196616 | tf_op jit(solution)/shard_map/ppermute | solution.py:963
  261.6 2.0 copy-start
  261.6 4.9 %collective-permute-start.34 = (f32[1472,256]{1,0:T(8,128)S(1)}, f32[1472,256]{1,0:T(8,128)S(1)}, u32[]{:S(2)}, u32[]{:S(2)}) collective-permute-start(f32[1472,256]{1,0:T(8,128)S(1)} %pad_maximum_fusion.1.refs_1_), channel_id=1, source_target_pairs={{0,2},{2,0},{4,6},{6,4},{8,10},{10,8},{12,14},{14,12},{16,18},{18,... | collective-permute-start | bytes 4521992 | tf_op jit(solution)/shard_map/ppermute | solution.py:963
  263.3 7.1 %copy-start.1 = (f32[1472,256]{1,0:T(8,128)}, f32[1472,256]{1,0:T(8,128)S(1)}, u32[]{:S(2)}) copy-start(f32[1472,256]{1,0:T(8,128)S(1)} %pad_maximum_fusion.refs_0_) | copy-start | bytes 4521988
  263.4 3.8 %collective-permute-start.33 = (f32[1472,256]{1,0:T(8,128)S(1)}, f32[1472,256]{1,0:T(8,128)S(1)}, u32[]{:S(2)}, u32[]{:S(2)}) collective-permute-start(f32[1472,256]{1,0:T(8,128)S(1)} %pad_maximum_fusion.refs_0_), channel_id=1, source_target_pairs={{0,2},{2,0},{4,6},{6,4},{8,10},{10,8},{12,14},{14,12},{16,18},{18,... | collective-permute-start | bytes 4521992 | tf_op jit(solution)/shard_map/ppermute | solution.py:963
  263.5 14.4 %collective-permute-start.29 = (f32[384,256]{1,0:T(8,128)S(1)}, f32[384,256]{1,0:T(8,128)}, u32[]{:S(2)}, u32[]{:S(2)}) collective-permute-start(f32[384,256]{1,0:T(8,128)S(1)} %pad_maximum_fusion.8), channel_id=1, source_target_pairs={{0,1},{1,0},{2,3},{3,2},{4,5},{5,4},{6,7},{7,6},{8,9},{9,8},{10,11... | collective-permute-start | bytes 1179656 | tf_op jit(solution)/shard_map/ppermute | solution.py:965
  265.3 12.7 %collective-permute-start.28 = (f32[384,256]{1,0:T(8,128)S(1)}, f32[384,256]{1,0:T(8,128)}, u32[]{:S(2)}, u32[]{:S(2)}) collective-permute-start(f32[384,256]{1,0:T(8,128)S(1)} %pad_maximum_fusion.7), channel_id=1, source_target_pairs={{0,4},{2,6},{4,0},{6,2},{8,12},{10,14},{12,8},{14,10},{16,20},{18,... | collective-permute-start | bytes 1179656 | tf_op jit(solution)/shard_map/ppermute | solution.py:963
  265.8 12.1 %collective-permute-start.30 = (f32[32,512]{1,0:T(8,128)S(1)}, f32[32,512]{1,0:T(8,128)S(1)}, u32[]{:S(2)}, u32[]{:S(2)}) collective-permute-start(f32[32,512]{1,0:T(8,128)S(1)} %add.330), channel_id=1, source_target_pairs={{0,1},{1,0},{2,3},{3,2},{4,5},{5,4},{6,7},{7,6},{8,9},{9,8},{10,11... | collective-permute-start | bytes 196616 | tf_op jit(solution)/shard_map/ppermute | solution.py:965
  266.5 11.4 %collective-permute-start.31 = (f32[32,512]{1,0:T(8,128)S(1)}, f32[32,512]{1,0:T(8,128)S(1)}, u32[]{:S(2)}, u32[]{:S(2)}) collective-permute-start(f32[32,512]{1,0:T(8,128)S(1)} %add.330), channel_id=1, source_target_pairs={{0,8},{2,10},{4,12},{6,14},{8,0},{10,2},{12,4},{14,6},{16,24},{18,... | collective-permute-start | bytes 196616 | tf_op jit(solution)/shard_map/ppermute | solution.py:963
  268.8 9.2 %collective-permute-start.32 = (f32[32,512]{1,0:T(8,128)S(1)}, f32[32,512]{1,0:T(8,128)S(1)}, u32[]{:S(2)}, u32[]{:S(2)}) collective-permute-start(f32[32,512]{1,0:T(8,128)S(1)} %add.330), channel_id=1, source_target_pairs={{0,9},{1,8},{2,11},{3,10},{4,13},{5,12},{6,15},{7,14},{8,1},{9,0},... | collective-permute-start | bytes 196616 | tf_op jit(solution)/shard_map/ppermute | solution.py:968
  279.0 6.0 %copy-start.2 = (f32[768,256]{1,0:T(8,128)}, f32[768,256]{1,0:T(8,128)S(1)}, u32[]{:S(2)}) copy-start(f32[768,256]{1,0:T(8,128)S(1)} %pad_maximum_fusion.3.refs_1_) | copy-start | bytes 2359300
  279.0 6.0 %collective-permute-start.37 = (f32[768,256]{1,0:T(8,128)S(1)}, f32[768,256]{1,0:T(8,128)S(1)}, u32[]{:S(2)}, u32[]{:S(2)}) collective-permute-start(f32[768,256]{1,0:T(8,128)S(1)} %pad_maximum_fusion.3.refs_1_), channel_id=1, source_target_pairs={{0,2},{2,0},{4,6},{6,4},{8,10},{10,8},{12,14},{14,12},{16,18},{18,... | collective-permute-start | bytes 2359304 | tf_op jit(solution)/shard_map/ppermute | solution.py:963
  280.3 4.6 %copy-start.3 = (f32[768,256]{1,0:T(8,128)}, f32[768,256]{1,0:T(8,128)S(1)}, u32[]{:S(2)}) copy-start(f32[768,256]{1,0:T(8,128)S(1)} %pad_maximum_fusion.2.refs_0_) | copy-start | bytes 2359300
  280.3 4.6 %collective-permute-start.36 = (f32[768,256]{1,0:T(8,128)S(1)}, f32[768,256]{1,0:T(8,128)}, u32[]{:S(2)}, u32[]{:S(2)}) collective-permute-start(f32[768,256]{1,0:T(8,128)S(1)} %pad_maximum_fusion.2.refs_0_), channel_id=1, source_target_pairs={{0,2},{2,0},{4,6},{6,4},{8,10},{10,8},{12,14},{14,12},{16,18},{18,... | collective-permute-start | bytes 2359304 | tf_op jit(solution)/shard_map/ppermute | solution.py:963
  281.5 8.9 %collective-permute-start.35 = (f32[32,512]{1,0:T(8,128)S(1)}, f32[32,512]{1,0:T(8,128)S(1)}, u32[]{:S(2)}, u32[]{:S(2)}) collective-permute-start(f32[32,512]{1,0:T(8,128)S(1)} %add_add_fusion.4), channel_id=1, source_target_pairs={{0,16},{2,18},{4,20},{6,22},{8,24},{10,26},{12,28},{14,30},{16,0},... | collective-permute-start | bytes 196616 | tf_op jit(solution)/shard_map/ppermute | solution.py:963
  (6 other events, 6.0 us)
where the time goes:
time: 294 us; the launch traced here: 293 us
  Pallas kernels  205 us (70%)
  starting transfers between devices  39.9 us (14%)
  other arithmetic  25.3 us (9%)
  waiting for transfers between devices  15.1 us (5%)
  local copies, waits for them, and re-layouts  6.08 us (2%)
    pallas_call x1, Pallas kernels, run_head(): pl.pallas_call(head_kernel, grid_spec=pltpu.PrefetchScalarGridSpec(num_sc...  85.7 us
    pallas_call x2, Pallas kernels, run_up(): pl.pallas_call(up_kernel, grid=(count // rows,), in_specs=in_specs + [pl....  33.6 us
    pallas_call x2, Pallas kernels, run_norm(): pl.pallas_call(functools.partial(norm_kernel, [pair[0].shape[1] for pair...  23.3 us
    ppermute x24, starting transfers between devices, exchange(): lax.ppermute(value, 'clip', [(i, i ^ across['clip']) for i in range(lax.a...  20 us
    pallas_call x2, Pallas kernels, run_wave(): pl.pallas_call(functools.partial(wave_kernel, first_blk, count // clips,...  19.7 us
    pallas_call x1, Pallas kernels, run_down(): pl.pallas_call(down_kernel, grid=(count // rows,), in_specs=[pl.BlockSpec...  15.4 us
    add x8, other arithmetic, added(): sum((lax.dynamic_slice(v, (row, col), (rows, cols)) for v, row, col in te...  14 us
    pallas_call x2, Pallas kernels, run_conv(): pl.pallas_call(functools.partial(conv_kernel, clip), grid_spec=pltpu.Pref...  13.8 us
  transfers between devices with their start and end apart: 38, of which 6 were waited for; matrix products, arithmetic and copies ran while one was open for 5% of the time, Pallas kernels for 35%

commit v1 on v0

--- a/solution.py
+++ b/solution.py
@@ -161,15 +161,11 @@
     o_istd,
     o_adt_h,
     o_adt_l,
-    o_act_h,
-    o_act_l,
     o_slope,
     o_spec,
     o_gm,
     o_gb_h,
     o_gb_l,
-    o_gbt_h,
-    o_gbt_l,
     o_keep,
     o_send,
     o_small,
@@ -190,6 +186,9 @@
     gm4,
     gl_h,
     gl_l,
+    act_h,
+    act_l,
+    acc_gdn,
     acc_ghw,
     acc_ghb,
     acc_ghwe,
@@ -230,7 +229,7 @@
         ext_w[0:1, :] = head_wt[half : half + 1, :]
         ext_w[1:2, :] = head_wt[nfft + 1 : nfft + 2, :]
         ext_w[2:8, :] = jnp.zeros((6, width), F32)
-        for ref in (acc_ghw, acc_ghb, acc_ghwe, acc_ghbe, acc_gls, acc_gmb):
+        for ref in (acc_gdn, acc_ghw, acc_ghb, acc_ghwe, acc_ghbe, acc_gls, acc_gmb):
             ref[...] = jnp.zeros_like(ref)
 
     base = pl.multiple_of(blk * ROWS, ROWS)
@@ -329,8 +328,8 @@
         cdf = 0.5 + 0.5 * lax.erf(upward * np.float32(0.7071067811865476))
         density = jnp.exp(upward * upward * -0.5) * np.float32(0.3989422804014327)
         o_slope[:, cols] = cdf + upward * density
-        o_act_h[:, cols], o_act_l[:, cols] = split(upward * cdf)
-    branch = dot3((o_act_h[...], o_act_l[...]), (down_h[...], down_l[...])) + down_b[...].reshape(1, width)
+        act_h[:, cols], act_l[:, cols] = split(upward * cdf)
+    branch = dot3((act_h[...], act_l[...]), (down_h[...], down_l[...])) + down_b[...].reshape(1, width)
     scale = layer_scale[...].reshape(1, width)
     residual = by_parity(pad4, rows8) + scale * branch
     res = split(residual)
@@ -409,7 +408,7 @@
     grad_branch = grad_mixed * scale
     gb = split(grad_branch)
     o_gb_h[...], o_gb_l[...] = gb
-    o_gbt_h[...], o_gbt_l[...] = gb[0].T, gb[1].T
+    acc_gdn[...] += dot3((gb[0].T, gb[1].T), (act_h[...], act_l[...]))
 
     @pl.when((clip == clips - 1) & (blk == blks - 1))
     def _():
@@ -434,8 +433,11 @@
                     lanes = slice(t * LANES, (t + 1) * LANES)
                     for ref, at in ((o_keep, first), (o_send, half + 1 - first)):
                         ref[0 : half + 1, lanes] = head4[t, at : at + half + 1, :]
-                        ref[half + 1 :, lanes] = jnp.zeros((ref.shape[0] - half - 1, LANES), F32)
-
+                        ref[half + 1 : HEAD_ROWS, lanes] = jnp.zeros((HEAD_ROWS - half - 1, LANES), F32)
+
+        rows = hidden // 2
+        for ref, part in ((o_keep, core), (o_send, 1 - core)):
+            ref[HEAD_ROWS:, :] = acc_gdn[:, pl.ds(pl.multiple_of(part * rows, rows), rows)].T
         o_small[...] = jnp.zeros_like(o_small)
         for c in range(0, nfft, LANES):
             o_small[0:1, c : c + LANES] = bias4[c : c + LANES, :].T[0:1, :]
@@ -494,17 +496,13 @@
         row_out(LANES, F32),
         col_out,
         col_out,
-        row_out(hidden, BF16),
-        row_out(hidden, BF16),
         row_out(hidden, F32),
         row_out(nfft, F32),
         row_out(width, F32),
         row_out(width, BF16),
         row_out(width, BF16),
-        col_out,
-        col_out,
-        (SDS((HEAD_ROWS + hidden // 2, width), F32), whole((HEAD_ROWS, width))),
-        (SDS((HEAD_ROWS + hidden // 2, width), F32), whole((HEAD_ROWS, width))),
+        (SDS((HEAD_ROWS + hidden // 2, width), F32), fixed((HEAD_ROWS + hidden // 2, width))),
+        (SDS((HEAD_ROWS + hidden // 2, width), F32), fixed((HEAD_ROWS + hidden // 2, width))),
         (SDS((8, hidden), F32), whole((8, hidden))),
     ]
     wave_tiles = nfft // 2 // LANES
@@ -524,6 +522,9 @@
         pltpu.VMEM((tiles, ROWS, LANES), F32),
         pltpu.VMEM((ROWS, nfft), BF16),
         pltpu.VMEM((ROWS, nfft), BF16),
+        pltpu.VMEM((ROWS, hidden), BF16),
+        pltpu.VMEM((ROWS, hidden), BF16),
+        pltpu.VMEM((width, hidden), F32),
         pltpu.VMEM((width, nfft), F32),
         pltpu.VMEM((8, nfft), F32),
         pltpu.VMEM((8, width), F32),
@@ -545,53 +546,6 @@
         cost_estimate=pl.CostEstimate(flops=80_000_000_000, bytes_accessed=90_000_000, transcendentals=0),
         name="head",
     )(bands, offsets, x, x, x, edge, cot, cot, cot_edge, *operands)
-
-
-def down_kernel(gbt_h, gbt_l, act_h, act_l, *refs):
-    o_keep, o_send, acc, keep, send, sems = refs[-6:]
-    step = pl.program_id(0)
-
-    @pl.when(step == 0)
-    def _():
-        acc[...] = jnp.zeros_like(acc)
-
-    acc[...] += dot3((gbt_h[...], gbt_l[...]), (act_h[...], act_l[...]))
-
-    @pl.when(step == pl.num_programs(0) - 1)
-    def _():
-        core = lax.axis_index("clip") % 2
-        rows = keep.shape[0]
-        copies = []
-        for i, (ref, out, half) in enumerate(((keep, o_keep, core), (send, o_send, 1 - core))):
-            mine = pl.ds(pl.multiple_of(half * rows, rows), rows)
-            ref[...] = acc[:, mine].T
-            above = out.shape[0] - rows
-            copies.append(pltpu.make_async_copy(ref, out.at[pl.ds(above, rows), :], sems.at[i]))
-            copies[-1].start()
-        for copy in copies:
-            copy.wait()
-
-
-def run_down(gbt, act, keep, send):
-    width, count = gbt[0].shape
-    hidden = act[0].shape[1]
-    rows = 512
-    any_spec = pl.BlockSpec(memory_space=pl.ANY)
-    half = pltpu.VMEM((hidden // 2, width), F32)
-    return pl.pallas_call(
-        down_kernel,
-        grid=(count // rows,),
-        in_specs=[pl.BlockSpec((width, rows), lambda i: (0, i))] * 2
-        + [pl.BlockSpec((rows, hidden), lambda i: (i, 0))] * 2
-        + [any_spec] * 2,
-        out_specs=[any_spec] * 2,
-        out_shape=[SDS(keep.shape, F32), SDS(send.shape, F32)],
-        input_output_aliases={4: 0, 5: 1},
-        scratch_shapes=[pltpu.VMEM((width, hidden), F32), half, half, pltpu.SemaphoreType.DMA((2,))],
-        compiler_params=pltpu.CompilerParams(vmem_limit_bytes=VMEM),
-        cost_estimate=pl.CostEstimate(flops=10_000_000_000, bytes_accessed=20_000_000, transcendentals=0),
-        name="down_grads",
-    )(*gbt, *act, keep, send)
 
 
 def up_kernel(gb_h, gb_l, slope, adt_h, adt_l, down_w, *refs):
@@ -1057,9 +1011,11 @@
         (came,) = yield [(value, level)]
         value = jnp.concatenate([jnp.where(s == 0, value, came), jnp.where(s == 0, came, value)])
     parts = [value[:rows], value[rows:]]
-    for i in (1, 0):
-        came = yield [(part, order[i]) for part, order in zip(parts, orders)]
-        parts = [jnp.concatenate(pair) for pair in zip(parts, came)]
+    came = yield [(part, order[1]) for part, order in zip(parts, orders)]
+    parts = [jnp.concatenate(pair) for pair in zip(parts, came)]
+    came = yield [(part, order[0]) for part, order in zip(parts, orders)]
+    parts, came = lax.optimization_barrier((parts, came))
+    parts = [piece for pair in zip(parts, came) for piece in pair]
     others = yield [(part, core) for part in parts]
     return parts, others, orders
 
@@ -1083,18 +1039,20 @@
 def natural_blocks(orders, refs, copy):
     core = side(levels()[0])
     cols = refs[0].shape[1]
-    rows = refs[0].shape[0] // 4
+    rows = refs[0].shape[0] // 2
     for half in range(2):
-        for here, pair in ((core == half, refs[:2]), (core != half, refs[2:])):
-
-            @pl.when(here)
-            def _(pair=pair, half=half):
-                for i, (ref, order) in enumerate(zip(pair, orders)):
-                    a, b = (side(level) for level in order)
-                    for block in range(4):
-                        first = (2 * jnp.bitwise_xor(block // 2, a) + jnp.bitwise_xor(block % 2, b)) * rows
-                        value = ref[pl.ds(pl.multiple_of(first, 8), rows), :]
-                        copy(half, slice(i * cols, (i + 1) * cols), block * rows, value)
+        for here, four in ((core == half, refs[:4]), (core != half, refs[4:])):
+            for i, order in enumerate(orders):
+                a, b = (side(level) for level in order)
+                for top in range(2):
+                    for piece in range(2):
+
+                        @pl.when(here & (jnp.bitwise_xor(top, a) == piece))
+                        def _(ref=four[2 * i + piece], half=half, i=i, top=top, b=b):
+                            for low in range(2):
+                                first = pl.multiple_of(jnp.bitwise_xor(low, b) * rows, 8)
+                                value = ref[pl.ds(first, rows), :]
+                                copy(half, slice(i * cols, (i + 1) * cols), (2 * top + low) * rows, value)
 
 
 def to_runs(runs):
@@ -1116,7 +1074,7 @@
             (HEAD_ROWS, o_down, lambda half: half * (o_down.shape[0] // 2), o_down.shape[0] // 2),
         )
     )
-    natural_blocks(orders, refs[:4], copy)
+    natural_blocks(orders, refs[:8], copy)
 
 
 def up_order_kernel(orders, *refs):
@@ -1127,7 +1085,7 @@
         runs.append((at, up_t, lambda half, size=size, part=part: size * part + half * (size // 2), size // 2))
         at += size // 2
     copy = to_runs(runs)
-    natural_blocks(orders, refs[:4], copy)
+    natural_blocks(orders, refs[:8], copy)
     for c in range(0, up_t.shape[0], LANES):
         o_up[:, c : c + LANES] = up_t[c : c + LANES, :].T
 
@@ -1137,7 +1095,7 @@
     parts = after(waits, parts)
     return pl.pallas_call(
         functools.partial(kernel, orders),
-        in_specs=[pl.BlockSpec(memory_space=pltpu.VMEM)] * 4,
+        in_specs=[pl.BlockSpec(memory_space=pltpu.VMEM)] * 8,
         out_shape=out_shape,
         scratch_shapes=list(scratch),
         compiler_params=pltpu.CompilerParams(vmem_limit_bytes=VMEM),
@@ -1218,12 +1176,11 @@
         head_bias,
     )
     (
-        norm, istd, adt_h, adt_l, act_h, act_l, slope, spec, gm, gb_h, gb_l, gbt_h, gbt_l, hg_keep, hg_send, small,
+        norm, istd, adt_h, adt_l, slope, spec, gm, gb_h, gb_l, keep, send, small,
     ) = run_head(
         band_ids, offsets, inputs, edge, to_chunks(wave_cotangent), cot_edge, weights, jnp.asarray(turns), consts
     )
 
-    keep, send = run_down((gbt_h, gbt_l), (act_h, act_l), hg_keep, hg_send)
     sums = Sums()
     first_total = sums.add(halves_steps(keep, send, True))
     blks = frames // ROWS

time: 294 us -> 283 us (0.963)
  other arithmetic: 25.3 us -> 18.6 us
  Pallas kernels: 205 us -> 201 us
  starting transfers between devices: 39.9 us -> 43.1 us
    pallas_call x1 -> x0, Pallas kernels: 15.4 us -> none  [run_down(): pl.pallas_call(down_kernel, grid=(count // rows,), in_specs=[pl.BlockSpec...]
    pallas_call x1, Pallas kernels: 85.7 us -> 97.4 us  [run_head(): pl.pallas_call(head_kernel, grid_spec=pltpu.PrefetchScalarGridSpec(num_sc...]
    concatenate x8 -> x4, other arithmetic: 7.11 us -> 1.08 us  [halves_steps(): parts = [jnp.concatenate(pair) for pair in zip(parts, came)]]
    ppermute x24 -> x28, starting transfers between devices: 20 us -> 22.8 us  [exchange(): lax.ppermute(value, 'clip', [(i, i ^ across['clip']) for i in range(lax.a...]
    ppermute x24 -> x28, waiting for transfers between devices: 9.49 us -> 8.56 us  [exchange(): lax.ppermute(value, 'clip', [(i, i ^ across['clip']) for i in range(lax.a...]
  transfers between devices with their start and end apart: 38 -> 42, of which waited for: 6 -> 8; matrix products, arithmetic and copies ran while one was open for 5% -> 4% of each run, Pallas kernels for 35% -> 36%
where the time goes in v1:
time: 283 us; the launch traced here: 282 us
  Pallas kernels  201 us (71%)
  starting transfers between devices  43.1 us (15%)
  other arithmetic  18.6 us (7%)
  waiting for transfers between devices  13 us (5%)
  local copies, waits for them, and re-layouts  4.45 us (2%)
    pallas_call x1, Pallas kernels, run_head(): pl.pallas_call(head_kernel, grid_spec=pltpu.PrefetchScalarGridSpec(num_sc...  97.4 us
    pallas_call x2, Pallas kernels, run_up(): pl.pallas_call(up_kernel, grid=(count // rows,), in_specs=in_specs + [pl....  33.7 us
    pallas_call x2, Pallas kernels, run_norm(): pl.pallas_call(functools.partial(norm_kernel, [pair[0].shape[1] for pair...  23.1 us
    ppermute x28, starting transfers between devices, exchange(): lax.ppermute(value, 'clip', [(i, i ^ across['clip']) for i in range(lax.a...  22.8 us
    pallas_call x2, Pallas kernels, run_wave(): pl.pallas_call(functools.partial(wave_kernel, first_blk, count // clips,...  19.9 us
    pallas_call x2, Pallas kernels, run_conv(): pl.pallas_call(functools.partial(conv_kernel, clip), grid_spec=pltpu.Pref...  13.8 us
    add x8, other arithmetic, added(): sum((lax.dynamic_slice(v, (row, col), (rows, cols)) for v, row, col in te...  13.4 us
    ppermute x10, starting transfers between devices, exchange(): lax.ppermute(value, 'tm', [(i, i ^ across['tm']) for i in range(lax.axis_...  11.8 us
  transfers between devices with their start and end apart: 42, of which 8 were waited for; matrix products, arithmetic and copies ran while one was open for 4% of the time, Pallas kernels for 36%

profile of v1, /device:TPU:0, one launch (start us, length us, event | category | flops | bytes accessed | tf_op | source)
XLA Modules:
  0.0 282.1 jit_solution(6380396056543939222)
XLA Ops:
  1.4 3.0 %collective-permute-start.1 = (f32[2,8,640]{2,1,0:T(8,128)S(1)}, f32[2,8,640]{2,1,0:T(8,128)S(1)}, u32[]{:S(2)}, u32[]{:S(2)}) collective-permute-start(f32[2,8,640]{2,1,0:T(8,128)S(1)} %pad.4), channel_id=1, source_target_pairs={{0,1},{1,0},{2,3},{3,2},{4,5},{5,4},{6,7},{7,6},{8,9},{9,8},{10,11... | collective-permute-start | bytes 122888 | tf_op jit(solution)/shard_map/ppermute | solution.py:1158
  5.2 3.9 %collective-permute-done.edge_ref = f32[2,8,512]{2,1,0:T(8,128)S(1)} collective-permute-done((f32[2,8,512]{2,1,0:T(8,128)S(1)}, f32[2,8,512]{2,1,0:T(8,128)S(1)}, u32[]{:S(2)}, u32[]{:S(2)}) %collective-permute-start) | collective-permute-done | bytes 32800 | tf_op jit(solution)/shard_map/ppermute | solution.py:1158
  9.7 97.4 %head.1 = (f32[2048,512]{1,0:T(8,128)}, f32[2048,128]{1,0:T(8,128)}, bf16[512,2048]{1,0:T(8,128)(2,1)}, bf16[512,2048]{1,0:T(8,128)(2,1)}, f32[2048,1536]{1,0:T(...) custom-call(s32[2]{0:T(128)} %bands.5, s32[2]{0:T(128)} %offsets.9, ...), custom_call_target="tpu_custom_call" | custom-call | flops 80000000000 | bytes 90000000 | tf_op jit(solution)/shard_map/head/pallas_call | solution.py:535
  107.3 5.6 %collective-permute-done.2 = f32[1472,512]{1,0:T(8,128)S(1)} collective-permute-done((f32[1472,512]{1,0:T(8,128)}, f32[1472,512]{1,0:T(8,128)S(1)}, u32[]{:S(2)}, u32[]{:S(2)}) %collective-permute-start.2) | collective-permute-done | bytes 3014688 | tf_op jit(solution)/shard_map/ppermute | solution.py:917
  112.9 3.8 %dynamic-slice_add_fusion = (f32[736,256]{1,0:T(8,128)}, f32[736,256]{1,0:T(8,128)}) fusion(f32[1472,512]{1,0:T(8,128)S(1)} %collective-permute-done.2, s32[]{:T(128)S(6)} %select_n.186, f32[1472,512]{1,0:T(8,128)} %get-tuple-element.142, s32[]{:T(128)S(6)} %select_n.185), kind=kLoop, calls=%fused_computation.8 | loop fusion | flops 376832 | bytes 4521992 | tf_op jit(solution)/shard_map/add | solution.py:990
  116.7 1.5 collective-permute-start.3
  118.7 21.2 %up_grads.2 = (f32[768,512]{1,0:T(8,128)}, f32[768,512]{1,0:T(8,128)}, f32[1,1024]{1,0:T(1,128)}, bf16[2048,1024]{1,0:T(8,128)(2,1)}, bf16[2048,1024]{1,0:T(8,128)(2,1)}) custom-call(bf16[2048,512]{1,0:T(8,128)(2,1)} %get-tuple-element.144.gb_h, bf16[2048,512]{1,0:T(8,128)(2,1)} %get-tuple-element.145.gb_l, f32[2048,1536]{1,0:T(8,128)} %get-tuple-element.157.slope, ...), custom_call_target="tpu_custom_call" | custom-call | flops 10000000000 | bytes 20000000 | tf_op jit(solution)/shard_map/up_grads/pallas_call | solution.py:593
  139.9 1.5 dynamic-slice_add_fusion.4
  141.4 1.6 collective-permute-start.5
  143.5 12.5 %up_grads.3 = (f32[768,512]{1,0:T(8,128)}, f32[768,512]{1,0:T(8,128)}, f32[1,512]{1,0:T(1,128)}, bf16[2048,512]{1,0:T(8,128)(2,1)}, bf16[2048,512]{1,0:T(8,128)(2,1)}) custom-call(bf16[2048,512]{1,0:T(8,128)(2,1)} %get-tuple-element.144.gb_h, bf16[2048,512]{1,0:T(8,128)(2,1)} %get-tuple-element.145.gb_l, ...), custom_call_target="tpu_custom_call", output_to_operand_aliasing={{0}: (6, {}), {1}: (7, {})} | custom-call | flops 10000000000 | bytes 20000000 | tf_op jit(solution)/shard_map/up_grads/pallas_call | solution.py:593
  156.4 1.9 add_add_fusion
  158.2 0.9 fusion
  159.1 1.6 collective-permute-start.7
  160.7 1.2 dynamic-slice_add_fusion.2
  162.5 1.5 collective-permute-start.9
  164.0 11.6 %norm_grads.2 = (f32[1024,512]{1,0:T(8,128)}, f32[2,8,512]{2,1,0:T(8,128)}, f32[4,512]{1,0:T(4,128)}, f32[4,512]{1,0:T(4,128)}) custom-call(s32[2]{0:T(128)} %bands.5, bf16[2048,1024]{1,0:T(8,128)(2,1)} %get-tuple-element.169.refs_0_, bf16[2048,1024]{1,0:T(8,128)(2,1)} %get-tuple-element.170.refs_1_, bf16[2048,512]{1,0:T(8,128)(2,1)} %get-tuple-element.171.refs_2_, ...), custom_call_target="tpu_custom_call" | custom-call | flops 5000000000 | bytes 12000000 | tf_op jit(solution)/shard_map/norm_grads/pallas_call | solution.py:676
  175.6 1.1 dynamic-slice_add_fusion.6
  176.7 1.6 collective-permute-start.12
  178.9 1.7 fusion.2
  180.5 2.6 collective-permute-start.11
  183.1 11.5 %norm_grads.3 = (f32[1024,512]{1,0:T(8,128)}, f32[2,8,512]{2,1,0:T(8,128)}, f32[4,512]{1,0:T(4,128)}, f32[4,512]{1,0:T(4,128)}) custom-call(s32[2]{0:T(128)} %bands.5, bf16[2048,1024]{1,0:T(8,128)(2,1)} %get-tuple-element.169.refs_0_, bf16[2048,1024]{1,0:T(8,128)(2,1)} %get-tuple-element.170.refs_1_, bf16[2048,512]{1,0:T(8,128)(2,1)} %get-tuple-element.171.refs_2_, ...), custom_call_target="tpu_custom_call" | custom-call | flops 5000000000 | bytes 12000000 | tf_op jit(solution)/shard_map/norm_grads/pallas_call | solution.py:676
  194.6 1.1 add_add_fusion.3
  195.8 0.8 collective-permute-start.15
  196.7 1.1 fusion.5
  198.6 10.0 %wave.2 = (f32[5120,128]{1,0:T(8,128)}, f32[2,8,640]{2,1,0:T(8,128)}) custom-call(s32[2]{0:T(128)} %offsets.9, f32[2048,1280]{1,0:T(8,128)} %get-tuple-element.223.spec, bf16[512,512]{1,0:T(8,128)(2,1)} %constant.144.clone.t1h, bf16[512,512]{1,0:T(8,128)(2,1)} %constant.145.clone.t1l, bf16[512,512]{1,0:T(8,128)(2,1)} %constant.146.clone.t2h, ...), custom_call_target="tpu_custom_call" | custom-call | flops 5000000000 | bytes 8000000 | tf_op jit(solution)/shard_map/wave/pallas_call | solution.py:884
  208.7 0.8 collective-permute-done.15
  210.2 3.4 %collective-permute-start.18 = (f32[2,8,640]{2,1,0:T(8,128)S(1)}, f32[2,8,640]{2,1,0:T(8,128)S(1)}, u32[]{:S(2)}, u32[]{:S(2)}) collective-permute-start(f32[2,8,640]{2,1,0:T(8,128)S(1)} %copy-done.20), channel_id=1, source_target_pairs={{0,1},{2,3},{4,5},{6,7},{8,9},{10,11},{12,13},{14,15},{16,17},{18,... | collective-permute-start | bytes 122888 | tf_op jit(solution)/shard_map/ppermute | solution.py:912
  213.6 2.6 collective-permute-start.21
  216.2 6.7 %conv_grads.2 = (f32[2,1024,512]{2,1,0:T(8,128)}, f32[64,512]{1,0:T(8,128)}) custom-call(s32[2]{0:T(128)} %offsets.9, f32[2,1024,512]{2,1,0:T(8,128)} %x_down.5, f32[2,1024,512]{2,1,0:T(8,128)} %x_down.5, f32[2,1024,512]{2,1,0:T(8,128)} %x_down.5, f32[2,8,512]{2,1,0:T(8,128)} %copy-done.17, f32[1,1024,512]{2,1,0:T(8,128)} %bitcast.16, ...), custom_call_target="tpu_custom_call" | custom-call | flops 5000000000 | bytes 17000000 | tf_op jit(solution)/shard_map/conv_grads/pallas_call | solution.py:766
  223.3 2.9 %collective-permute-start.19 = (f32[368,256]{1,0:T(8,128)S(1)}, f32[368,256]{1,0:T(8,128)S(1)}, u32[]{:S(2)}, u32[]{:S(2)}) collective-permute-start(f32[368,256]{1,0:T(8,128)S(1)} %get-tuple-element.284), channel_id=1, source_target_pairs={{0,1},{1,0},{2,3},{3,2},{4,5},{5,4},{6,7},{7,6},{8,9},{9,8},{10,11... | collective-permute-start | bytes 1130504 | tf_op jit(solution)/shard_map/ppermute | solution.py:919
  226.2 1.5 collective-permute-start.20
  227.7 7.1 %conv_grads.3 = (f32[2,1024,512]{2,1,0:T(8,128)}, f32[64,512]{1,0:T(8,128)}) custom-call(s32[2]{0:T(128)} %offsets.9, f32[2,1024,512]{2,1,0:T(8,128)} %x_down.5, f32[2,1024,512]{2,1,0:T(8,128)} %x_down.5, f32[2,1024,512]{2,1,0:T(8,128)} %x_down.5, f32[2,8,512]{2,1,0:T(8,128)} %copy-done.17, ...), custom_call_target="tpu_custom_call", output_to_operand_aliasing={{0}: (12, {})} | custom-call | flops 5000000000 | bytes 17000000 | tf_op jit(solution)/shard_map/conv_grads/pallas_call | solution.py:766
  235.1 2.5 collective-permute-start.22
  237.6 1.6 pack.1
  239.3 2.0 collective-permute-start.24
  241.3 0.8 add.328
  242.2 2.1 collective-permute-start.27
  244.3 9.9 %wave.3 = (f32[5120,128]{1,0:T(8,128)}, f32[2,8,640]{2,1,0:T(8,128)}) custom-call(s32[2]{0:T(128)} %offsets.9, f32[2048,1280]{1,0:T(8,128)} %get-tuple-element.223.spec, bf16[512,512]{1,0:T(8,128)(2,1)} %constant.144.clone.t1h, bf16[512,512]{1,0:T(8,128)(2,1)} %constant.145.clone.t1l, ...), custom_call_target="tpu_custom_call", output_to_operand_aliasing={{0}: (11, {})} | custom-call | flops 5000000000 | bytes 8000000 | tf_op jit(solution)/shard_map/wave/pallas_call | solution.py:884
  254.1 1.4 collective-permute-done.27
  257.3 1.0 pad_maximum_fusion.3.refs_0_
  258.3 1.4 collective-permute-start.28
  260.0 1.5 collective-permute-start.30
  261.5 2.0 collective-permute-start.32
  263.6 0.8 slice.23
  264.4 5.8 %in_order.2 = (f32[1282,512]{1,0:T(8,128)}, f32[1536,512]{1,0:T(8,128)}) custom-call(f32[736,256]{1,0:T(8,128)} %copy-done.3, f32[736,256]{1,0:T(8,128)} %collective-permute-done.22.refs_1_, f32[736,256]{1,0:T(8,128)} %copy-done.2, f32[736,256]{1,0:T(8,128)} %copy-done.8, f32[736,256]{1,0:T(8,128)} %copy-done.9, f32[736,256]{1,0:T(8,128)} %copy-done.10, ...), custom_call_target="tpu_custom_call" | custom-call | tf_op jit(solution)/shard_map/in_order/pallas_call | solution.py:1096
  273.0 1.3 dynamic_update_slice.3
  275.2 4.7 %in_order.3 = f32[512,1536]{1,0:T(8,128)} custom-call(f32[384,256]{1,0:T(8,128)} %copy-done.5, f32[384,256]{1,0:T(8,128)} %copy-done.14, f32[384,256]{1,0:T(8,128)} %copy-done.4, f32[384,256]{1,0:T(8,128)} %copy-done.13, f32[384,256]{1,0:T(8,128)} %copy-done.15, f32[384,256]{1,0:T(8,128)} %copy-done.16, f32[384,256]{1,0:T(8,128)} %collective-permute-done.40.refs_6_, ...), custom_call_target="tpu_custom_call" | custom-call | tf_op jit(solution)/shard_map/in_order/pallas_call | solution.py:1096
  280.6 1.5 unpack.1
  (129 shorter events, 13.1 us)
Async XLA Ops:
  1.4 7.7 %collective-permute-start.1 = (f32[2,8,640]{2,1,0:T(8,128)S(1)}, f32[2,8,640]{2,1,0:T(8,128)S(1)}, u32[]{:S(2)}, u32[]{:S(2)}) collective-permute-start(f32[2,8,640]{2,1,0:T(8,128)S(1)} %pad.4), channel_id=1, source_target_pairs={{0,1},{1,0},{2,3},{3,2},{4,5},{5,4},{6,7},{7,6},{8,9},{9,8},{10,11... | collective-permute-start | bytes 122888 | tf_op jit(solution)/shard_map/ppermute | solution.py:1158
  5.2 3.9 %collective-permute-start = (f32[2,8,512]{2,1,0:T(8,128)S(1)}, f32[2,8,512]{2,1,0:T(8,128)S(1)}, u32[]{:S(2)}, u32[]{:S(2)}) collective-permute-start(f32[2,8,512]{2,1,0:T(8,128)S(1)} %slice_select_fusion), channel_id=1, source_target_pairs={{0,1},{1,0},{2,3},{3,2},{4,5},{5,4},{6,7},{7,6},{8,9},{9,8},{10,11... | collective-permute-start | bytes 98312 | tf_op jit(solution)/shard_map/ppermute | solution.py:1158
  107.1 5.7 %collective-permute-start.2 = (f32[1472,512]{1,0:T(8,128)}, f32[1472,512]{1,0:T(8,128)S(1)}, u32[]{:S(2)}, u32[]{:S(2)}) collective-permute-start(f32[1472,512]{1,0:T(8,128)} %get-tuple-element.143), channel_id=1, source_target_pairs={{0,2},{2,0},{4,6},{6,4},{8,10},{10,8},{12,14},{14,12},{16,18},{18,... | collective-permute-start | bytes 9043976 | tf_op jit(solution)/shard_map/ppermute | solution.py:917
  116.7 23.2 %collective-permute-start.3 = (f32[736,256]{1,0:T(8,128)}, f32[736,256]{1,0:T(8,128)}, u32[]{:S(2)}, u32[]{:S(2)}) collective-permute-start(f32[736,256]{1,0:T(8,128)} %get-tuple-element.276), channel_id=1, source_target_pairs={{0,4},{2,6},{4,0},{6,2},{8,12},{10,14},{12,8},{14,10},{16,20},{18,... | collective-permute-start | bytes 2261000 | tf_op jit(solution)/shard_map/ppermute | solution.py:917
  118.2 21.7 %collective-permute-start.4 = (f32[736,256]{1,0:T(8,128)}, f32[736,256]{1,0:T(8,128)}, u32[]{:S(2)}, u32[]{:S(2)}) collective-permute-start(f32[736,256]{1,0:T(8,128)} %get-tuple-element.275), channel_id=1, source_target_pairs={{0,1},{1,0},{2,3},{3,2},{4,5},{5,4},{6,7},{7,6},{8,9},{9,8},{10,11... | collective-permute-start | bytes 2261000 | tf_op jit(solution)/shard_map/ppermute | solution.py:919
  118.7 21.2 %copy-start = (f32[1472,512]{1,0:T(8,128)S(1)}, f32[1472,512]{1,0:T(8,128)}, u32[]{:S(2)}) copy-start(f32[1472,512]{1,0:T(8,128)} %get-tuple-element.142) | copy-start | bytes 9043972
  141.4 14.6 %collective-permute-start.5 = (f32[368,256]{1,0:T(8,128)S(1)}, f32[368,256]{1,0:T(8,128)}, u32[]{:S(2)}, u32[]{:S(2)}) collective-permute-start(f32[368,256]{1,0:T(8,128)S(1)} %get-tuple-element.274), channel_id=1, source_target_pairs={{0,1},{1,0},{2,3},{3,2},{4,5},{5,4},{6,7},{7,6},{8,9},{9,8},{10,11... | collective-permute-start | bytes 1130504 | tf_op jit(solution)/shard_map/ppermute | solution.py:919
  143.0 13.0 %collective-permute-start.6 = (f32[368,256]{1,0:T(8,128)S(1)}, f32[368,256]{1,0:T(8,128)}, u32[]{:S(2)}, u32[]{:S(2)}) collective-permute-start(f32[368,256]{1,0:T(8,128)S(1)} %get-tuple-element.273), channel_id=1, source_target_pairs={{0,4},{2,6},{4,0},{6,2},{8,12},{10,14},{12,8},{14,10},{16,20},{18,... | collective-permute-start | bytes 1130504 | tf_op jit(solution)/shard_map/ppermute | solution.py:917
  156.1 4.6 %collective-permute-start.8 = (f32[768,512]{1,0:T(8,128)}, f32[768,512]{1,0:T(8,128)}, u32[]{:S(2)}, u32[]{:S(2)}) collective-permute-start(f32[768,512]{1,0:T(8,128)} %get-tuple-element.168), channel_id=1, source_target_pairs={{0,2},{2,0},{4,6},{6,4},{8,10},{10,8},{12,14},{14,12},{16,18},{18,... | collective-permute-start | bytes 4718600 | tf_op jit(solution)/shard_map/ppermute | solution.py:917
  159.1 16.5 %collective-permute-start.7 = (f32[368,256]{1,0:T(8,128)}, f32[368,256]{1,0:T(8,128)}, u32[]{:S(2)}, u32[]{:S(2)}) collective-permute-start(f32[368,256]{1,0:T(8,128)} %fusion), channel_id=1, source_target_pairs={{0,8},{2,10},{4,12},{6,14},{8,0},{10,2},{12,4},{14,6},{16,24},{18,... | collective-permute-start | bytes 1130504 | tf_op jit(solution)/shard_map/ppermute | solution.py:917
  161.9 13.7 %collective-permute-start.10 = (f32[384,256]{1,0:T(8,128)S(1)}, f32[384,256]{1,0:T(8,128)S(1)}, u32[]{:S(2)}, u32[]{:S(2)}) collective-permute-start(f32[384,256]{1,0:T(8,128)S(1)} %get-tuple-element.281), channel_id=1, source_target_pairs={{0,1},{1,0},{2,3},{3,2},{4,5},{5,4},{6,7},{7,6},{8,9},{9,8},{10,11... | collective-permute-start | bytes 1179656 | tf_op jit(solution)/shard_map/ppermute | solution.py:919
  162.5 13.1 %collective-permute-start.9 = (f32[384,256]{1,0:T(8,128)S(1)}, f32[384,256]{1,0:T(8,128)S(1)}, u32[]{:S(2)}, u32[]{:S(2)}) collective-permute-start(f32[384,256]{1,0:T(8,128)S(1)} %get-tuple-element.282), channel_id=1, source_target_pairs={{0,4},{2,6},{4,0},{6,2},{8,12},{10,14},{12,8},{14,10},{16,20},{18,... | collective-permute-start | bytes 1179656 | tf_op jit(solution)/shard_map/ppermute | solution.py:917
  176.7 17.9 %collective-permute-start.12 = (f32[192,256]{1,0:T(8,128)S(1)}, f32[192,256]{1,0:T(8,128)S(1)}, u32[]{:S(2)}, u32[]{:S(2)}) collective-permute-start(f32[192,256]{1,0:T(8,128)S(1)} %get-tuple-element.280), channel_id=1, source_target_pairs={{0,1},{1,0},{2,3},{3,2},{4,5},{5,4},{6,7},{7,6},{8,9},{9,8},{10,11... | collective-permute-start | bytes 589832 | tf_op jit(solution)/shard_map/ppermute | solution.py:919
  178.3 16.3 %collective-permute-start.13 = (f32[192,256]{1,0:T(8,128)S(1)}, f32[192,256]{1,0:T(8,128)S(1)}, u32[]{:S(2)}, u32[]{:S(2)}) collective-permute-start(f32[192,256]{1,0:T(8,128)S(1)} %get-tuple-element.279), channel_id=1, source_target_pairs={{0,4},{2,6},{4,0},{6,2},{8,12},{10,14},{12,8},{14,10},{16,20},{18,... | collective-permute-start | bytes 589832 | tf_op jit(solution)/shard_map/ppermute | solution.py:917
  180.5 14.1 %collective-permute-start.11 = (f32[184,256]{1,0:T(8,128)}, f32[184,256]{1,0:T(8,128)}, u32[]{:S(2)}, u32[]{:S(2)}) collective-permute-start(f32[184,256]{1,0:T(8,128)} %fusion.2), channel_id=1, source_target_pairs={{0,16},{2,18},{4,20},{6,22},{8,24},{10,26},{12,28},{14,30},{16,0},... | collective-permute-start | bytes 565256 | tf_op jit(solution)/shard_map/ppermute | solution.py:917
  195.8 13.7 %collective-permute-start.15 = (f32[384,256]{1,0:T(8,128)S(1)}, f32[384,256]{1,0:T(8,128)S(1)}, u32[]{:S(2)}, u32[]{:S(2)}) collective-permute-start(f32[384,256]{1,0:T(8,128)S(1)} %pad_maximum_fusion.2), channel_id=1, source_target_pairs={{0,8},{2,10},{4,12},{6,14},{8,0},{10,2},{12,4},{14,6},{16,24},{18,... | collective-permute-start | bytes 1179656 | tf_op jit(solution)/shard_map/ppermute | solution.py:917
  197.7 11.0 %collective-permute-start.14 = (f32[184,256]{1,0:T(8,128)S(1)}, f32[184,256]{1,0:T(8,128)S(1)}, u32[]{:S(2)}, u32[]{:S(2)}) collective-permute-start(f32[184,256]{1,0:T(8,128)S(1)} %fusion.5), channel_id=1, source_target_pairs={{0,16},{2,18},{4,20},{6,22},{8,24},{10,26},{12,28},{14,30},{16,0},... | collective-permute-start | bytes 565256 | tf_op jit(solution)/shard_map/ppermute | solution.py:917
  198.1 10.5 %collective-permute-start.16 = (f32[2,8,512]{2,1,0:T(8,128)S(1)}, f32[2,8,512]{2,1,0:T(8,128)S(1)}, u32[]{:S(2)}, u32[]{:S(2)}) collective-permute-start(f32[2,8,512]{2,1,0:T(8,128)S(1)} %copy-done.22), channel_id=1, source_target_pairs={{0,1},{1,0},{2,3},{3,2},{4,5},{5,4},{6,7},{7,6},{8,9},{9,8},{10,11... | collective-permute-start | bytes 98312 | tf_op jit(solution)/shard_map/ppermute | solution.py:919
  209.7 13.6 %collective-permute-start.17 = (f32[368,256]{1,0:T(8,128)S(1)}, f32[368,256]{1,0:T(8,128)S(1)}, u32[]{:S(2)}, u32[]{:S(2)}) collective-permute-start(f32[368,256]{1,0:T(8,128)S(1)} %pad_maximum_fusion.5), channel_id=1, source_target_pairs={{0,8},{2,10},{4,12},{6,14},{8,0},{10,2},{12,4},{14,6},{16,24},{18,... | collective-permute-start | bytes 1130504 | tf_op jit(solution)/shard_map/ppermute | solution.py:917
  210.2 12.8 %collective-permute-start.18 = (f32[2,8,640]{2,1,0:T(8,128)S(1)}, f32[2,8,640]{2,1,0:T(8,128)S(1)}, u32[]{:S(2)}, u32[]{:S(2)}) collective-permute-start(f32[2,8,640]{2,1,0:T(8,128)S(1)} %copy-done.20), channel_id=1, source_target_pairs={{0,1},{2,3},{4,5},{6,7},{8,9},{10,11},{12,13},{14,15},{16,17},{18,... | collective-permute-start | bytes 122888 | tf_op jit(solution)/shard_map/ppermute | solution.py:912
  213.6 21.2 %collective-permute-start.21 = (f32[384,256]{1,0:T(8,128)S(1)}, f32[384,256]{1,0:T(8,128)S(1)}, u32[]{:S(2)}, u32[]{:S(2)}) collective-permute-start(f32[384,256]{1,0:T(8,128)S(1)} %fusion.6), channel_id=1, source_target_pairs={{0,16},{2,18},{4,20},{6,22},{8,24},{10,26},{12,28},{14,30},{16,0},... | collective-permute-start | bytes 1179656 | tf_op jit(solution)/shard_map/ppermute | solution.py:917
  223.0 11.8 %copy-start.19 = (f32[2,8,640]{2,1,0:T(8,128)}, f32[2,8,640]{2,1,0:T(8,128)S(1)}, u32[]{:S(2)}) copy-start(f32[2,8,640]{2,1,0:T(8,128)S(1)} %collective-permute-done.18.refs_0_) | copy-start | bytes 122884
  223.3 11.4 %collective-permute-start.19 = (f32[368,256]{1,0:T(8,128)S(1)}, f32[368,256]{1,0:T(8,128)S(1)}, u32[]{:S(2)}, u32[]{:S(2)}) collective-permute-start(f32[368,256]{1,0:T(8,128)S(1)} %get-tuple-element.284), channel_id=1, source_target_pairs={{0,1},{1,0},{2,3},{3,2},{4,5},{5,4},{6,7},{7,6},{8,9},{9,8},{10,11... | collective-permute-start | bytes 1130504 | tf_op jit(solution)/shard_map/ppermute | solution.py:919
  226.2 8.7 %collective-permute-start.20 = (f32[368,256]{1,0:T(8,128)S(1)}, f32[368,256]{1,0:T(8,128)S(1)}, u32[]{:S(2)}, u32[]{:S(2)}) collective-permute-start(f32[368,256]{1,0:T(8,128)S(1)} %get-tuple-element.283), channel_id=1, source_target_pairs={{0,4},{2,6},{4,0},{6,2},{8,12},{10,14},{12,8},{14,10},{16,20},{18,... | collective-permute-start | bytes 1130504 | tf_op jit(solution)/shard_map/ppermute | solution.py:917
  234.9 21.3 %copy-start.2 = (f32[736,256]{1,0:T(8,128)}, f32[736,256]{1,0:T(8,128)S(1)}, u32[]{:S(2)}) copy-start(f32[736,256]{1,0:T(8,128)S(1)} %pad_maximum_fusion.1.refs_2_) | copy-start | bytes 2260996
  235.0 20.6 %copy-start.3 = (f32[736,256]{1,0:T(8,128)}, f32[736,256]{1,0:T(8,128)S(1)}, u32[]{:S(2)}) copy-start(f32[736,256]{1,0:T(8,128)S(1)} %pad_maximum_fusion.refs_0_) | copy-start | bytes 2260996
  235.0 20.6 %collective-permute-start.23 = (f32[736,256]{1,0:T(8,128)S(1)}, f32[736,256]{1,0:T(8,128)S(1)}, u32[]{:S(2)}, u32[]{:S(2)}) collective-permute-start(f32[736,256]{1,0:T(8,128)S(1)} %pad_maximum_fusion.1.refs_2_), channel_id=1, source_target_pairs={{0,1},{1,0},{2,3},{3,2},{4,5},{5,4},{6,7},{7,6},{8,9},{9,8},{10,11... | collective-permute-start | bytes 2261000 | tf_op jit(solution)/shard_map/ppermute | solution.py:919
  235.1 20.5 %collective-permute-start.22 = (f32[736,256]{1,0:T(8,128)S(1)}, f32[736,256]{1,0:T(8,128)}, u32[]{:S(2)}, u32[]{:S(2)}) collective-permute-start(f32[736,256]{1,0:T(8,128)S(1)} %pad_maximum_fusion.refs_0_), channel_id=1, source_target_pairs={{0,4},{2,6},{4,0},{6,2},{8,12},{10,14},{12,8},{14,10},{16,20},{18,... | collective-permute-start | bytes 2261000 | tf_op jit(solution)/shard_map/ppermute | solution.py:917
  239.2 2.1 collective-permute-start.26
  239.3 16.3 %collective-permute-start.24 = (f32[192,256]{1,0:T(8,128)S(1)}, f32[192,256]{1,0:T(8,128)}, u32[]{:S(2)}, u32[]{:S(2)}) collective-permute-start(f32[192,256]{1,0:T(8,128)S(1)} %get-tuple-element.286), channel_id=1, source_target_pairs={{0,1},{1,0},{2,3},{3,2},{4,5},{5,4},{6,7},{7,6},{8,9},{9,8},{10,11... | collective-permute-start | bytes 589832 | tf_op jit(solution)/shard_map/ppermute | solution.py:919
  241.3 14.3 %collective-permute-start.25 = (f32[192,256]{1,0:T(8,128)S(1)}, f32[192,256]{1,0:T(8,128)S(1)}, u32[]{:S(2)}, u32[]{:S(2)}) collective-permute-start(f32[192,256]{1,0:T(8,128)S(1)} %get-tuple-element.285), channel_id=1, source_target_pairs={{0,4},{2,6},{4,0},{6,2},{8,12},{10,14},{12,8},{14,10},{16,20},{18,... | collective-permute-start | bytes 589832 | tf_op jit(solution)/shard_map/ppermute | solution.py:917
  242.2 13.4 %collective-permute-start.27 = (f32[32,512]{1,0:T(8,128)S(1)}, f32[32,512]{1,0:T(8,128)S(1)}, u32[]{:S(2)}, u32[]{:S(2)}) collective-permute-start(f32[32,512]{1,0:T(8,128)S(1)} %add.328), channel_id=1, source_target_pairs={{0,4},{2,6},{4,0},{6,2},{8,12},{10,14},{12,8},{14,10},{16,20},{18,... | collective-permute-start | bytes 196616 | tf_op jit(solution)/shard_map/ppermute | solution.py:917
  255.6 2.7 collective-permute-start.33
  255.7 4.3 %collective-permute-start.34 = (f32[736,256]{1,0:T(8,128)}, f32[736,256]{1,0:T(8,128)S(1)}, u32[]{:S(2)}, u32[]{:S(2)}) collective-permute-start(f32[736,256]{1,0:T(8,128)} %collective-permute-done.22.refs_1_), channel_id=1, source_target_pairs={{0,2},{2,0},{4,6},{6,4},{8,10},{10,8},{12,14},{14,12},{16,18},{18,... | collective-permute-start | bytes 2261000 | tf_op jit(solution)/shard_map/ppermute | solution.py:917
  256.2 5.3 %collective-permute-start.35 = (f32[736,256]{1,0:T(8,128)S(1)}, f32[736,256]{1,0:T(8,128)S(1)}, u32[]{:S(2)}, u32[]{:S(2)}) collective-permute-start(f32[736,256]{1,0:T(8,128)S(1)} %pad_maximum_fusion.1.refs_2_), channel_id=1, source_target_pairs={{0,2},{2,0},{4,6},{6,4},{8,10},{10,8},{12,14},{14,12},{16,18},{18,... | collective-permute-start | bytes 2261000 | tf_op jit(solution)/shard_map/ppermute | solution.py:917
  256.3 5.2 %collective-permute-start.36 = (f32[736,256]{1,0:T(8,128)S(1)}, f32[736,256]{1,0:T(8,128)S(1)}, u32[]{:S(2)}, u32[]{:S(2)}) collective-permute-start(f32[736,256]{1,0:T(8,128)S(1)} %collective-permute-done.23.refs_3_), channel_id=1, source_target_pairs={{0,2},{2,0},{4,6},{6,4},{8,10},{10,8},{12,14},{14,12},{16,18},{18,... | collective-permute-start | bytes 2261000 | tf_op jit(solution)/shard_map/ppermute | solution.py:917
  256.7 14.6 %copy-start.4 = (f32[384,256]{1,0:T(8,128)}, f32[384,256]{1,0:T(8,128)S(1)}, u32[]{:S(2)}) copy-start(f32[384,256]{1,0:T(8,128)S(1)} %pad_maximum_fusion.4.refs_2_) | copy-start | bytes 1179652
  256.7 14.0 %collective-permute-start.29 = (f32[384,256]{1,0:T(8,128)S(1)}, f32[384,256]{1,0:T(8,128)S(1)}, u32[]{:S(2)}, u32[]{:S(2)}) collective-permute-start(f32[384,256]{1,0:T(8,128)S(1)} %pad_maximum_fusion.4.refs_2_), channel_id=1, source_target_pairs={{0,1},{1,0},{2,3},{3,2},{4,5},{5,4},{6,7},{7,6},{8,9},{9,8},{10,11... | collective-permute-start | bytes 1179656 | tf_op jit(solution)/shard_map/ppermute | solution.py:919
  258.3 12.4 %copy-start.5 = (f32[384,256]{1,0:T(8,128)}, f32[384,256]{1,0:T(8,128)S(1)}, u32[]{:S(2)}) copy-start(f32[384,256]{1,0:T(8,128)S(1)} %pad_maximum_fusion.3.refs_0_) | copy-start | bytes 1179652
  258.3 12.4 %collective-permute-start.28 = (f32[384,256]{1,0:T(8,128)S(1)}, f32[384,256]{1,0:T(8,128)S(1)}, u32[]{:S(2)}, u32[]{:S(2)}) collective-permute-start(f32[384,256]{1,0:T(8,128)S(1)} %pad_maximum_fusion.3.refs_0_), channel_id=1, source_target_pairs={{0,4},{2,6},{4,0},{6,2},{8,12},{10,14},{12,8},{14,10},{16,20},{18,... | collective-permute-start | bytes 1179656 | tf_op jit(solution)/shard_map/ppermute | solution.py:917
  260.0 10.7 %collective-permute-start.30 = (f32[32,512]{1,0:T(8,128)S(1)}, f32[32,512]{1,0:T(8,128)S(1)}, u32[]{:S(2)}, u32[]{:S(2)}) collective-permute-start(f32[32,512]{1,0:T(8,128)S(1)} %add.330), channel_id=1, source_target_pairs={{0,1},{1,0},{2,3},{3,2},{4,5},{5,4},{6,7},{7,6},{8,9},{9,8},{10,11... | collective-permute-start | bytes 196616 | tf_op jit(solution)/shard_map/ppermute | solution.py:919
  261.5 9.2 %collective-permute-start.31 = (f32[32,512]{1,0:T(8,128)S(1)}, f32[32,512]{1,0:T(8,128)S(1)}, u32[]{:S(2)}, u32[]{:S(2)}) collective-permute-start(f32[32,512]{1,0:T(8,128)S(1)} %add.330), channel_id=1, source_target_pairs={{0,8},{2,10},{4,12},{6,14},{8,0},{10,2},{12,4},{14,6},{16,24},{18,... | collective-permute-start | bytes 196616 | tf_op jit(solution)/shard_map/ppermute | solution.py:917
  261.5 9.2 %collective-permute-start.32 = (f32[32,512]{1,0:T(8,128)S(1)}, f32[32,512]{1,0:T(8,128)S(1)}, u32[]{:S(2)}, u32[]{:S(2)}) collective-permute-start(f32[32,512]{1,0:T(8,128)S(1)} %add.330), channel_id=1, source_target_pairs={{0,9},{1,8},{2,11},{3,10},{4,13},{5,12},{6,15},{7,14},{8,1},{9,0},... | collective-permute-start | bytes 196616 | tf_op jit(solution)/shard_map/ppermute | solution.py:922
  270.8 3.6 %collective-permute-start.38 = (f32[384,256]{1,0:T(8,128)S(1)}, f32[384,256]{1,0:T(8,128)S(1)}, u32[]{:S(2)}, u32[]{:S(2)}) collective-permute-start(f32[384,256]{1,0:T(8,128)S(1)} %pad_maximum_fusion.3.refs_0_), channel_id=1, source_target_pairs={{0,2},{2,0},{4,6},{6,4},{8,10},{10,8},{12,14},{14,12},{16,18},{18,... | collective-permute-start | bytes 1179656 | tf_op jit(solution)/shard_map/ppermute | solution.py:917
  270.8 3.5 %collective-permute-start.39 = (f32[384,256]{1,0:T(8,128)S(1)}, f32[384,256]{1,0:T(8,128)S(1)}, u32[]{:S(2)}, u32[]{:S(2)}) collective-permute-start(f32[384,256]{1,0:T(8,128)S(1)} %collective-permute-done.28.refs_1_), channel_id=1, source_target_pairs={{0,2},{2,0},{4,6},{6,4},{8,10},{10,8},{12,14},{14,12},{16,18},{18,... | collective-permute-start | bytes 1179656 | tf_op jit(solution)/shard_map/ppermute | solution.py:917
  271.3 3.0 %collective-permute-start.40 = (f32[384,256]{1,0:T(8,128)S(1)}, f32[384,256]{1,0:T(8,128)}, u32[]{:S(2)}, u32[]{:S(2)}) collective-permute-start(f32[384,256]{1,0:T(8,128)S(1)} %pad_maximum_fusion.4.refs_2_), channel_id=1, source_target_pairs={{0,2},{2,0},{4,6},{6,4},{8,10},{10,8},{12,14},{14,12},{16,18},{18,... | collective-permute-start | bytes 1179656 | tf_op jit(solution)/shard_map/ppermute | solution.py:917
  271.4 2.9 %collective-permute-start.41 = (f32[384,256]{1,0:T(8,128)S(1)}, f32[384,256]{1,0:T(8,128)}, u32[]{:S(2)}, u32[]{:S(2)}) collective-permute-start(f32[384,256]{1,0:T(8,128)S(1)} %collective-permute-done.29.refs_3_), channel_id=1, source_target_pairs={{0,2},{2,0},{4,6},{6,4},{8,10},{10,8},{12,14},{14,12},{16,18},{18,... | collective-permute-start | bytes 1179656 | tf_op jit(solution)/shard_map/ppermute | solution.py:917
  271.9 8.1 %collective-permute-start.37 = (f32[32,512]{1,0:T(8,128)S(1)}, f32[32,512]{1,0:T(8,128)S(1)}, u32[]{:S(2)}, u32[]{:S(2)}) collective-permute-start(f32[32,512]{1,0:T(8,128)S(1)} %add_add_fusion.4), channel_id=1, source_target_pairs={{0,16},{2,18},{4,20},{6,22},{8,24},{10,26},{12,28},{14,30},{16,0},... | collective-permute-start | bytes 196616 | tf_op jit(solution)/shard_map/ppermute | solution.py:917
  (17 other events, 64.3 us)

commit v2 on v1

--- a/solution.py
+++ b/solution.py
@@ -39,6 +39,13 @@
 
 def dot3(a, b, dims=NN):
     return dot(a[0], b[0], dims) + (dot(a[0], b[1], dims) + dot(a[1], b[0], dims))
+
+
+def dot3_few(a, b, dims=NN):
+    n = a.shape[0]
+    high = a.astype(BF16).astype(F32)
+    both = dot(jnp.concatenate([high, a - high], 0).astype(BF16), b[0], dims)
+    return both[:n] + (both[n:] + dot(high.astype(BF16), b[1], dims))
 
 
 def fold8(x):
@@ -336,8 +343,7 @@
     res_t = res[0].T, res[1].T
 
     bias = head_b[...].reshape(1, nfft + 2)
-    ext = split(ext_w[...])
-    ext_logits = dot3(ext, res, NT)
+    ext_logits = dot3_few(ext_w[...], res, NT)
     lane = lax.broadcasted_iota(jnp.int32, (1, ROWS), 1)
     ext_frame = base + jnp.where(lane < PAIRS, 2 * lane, 2 * (lane - PAIRS) + 1)
     ext_present = ext_frame >= local
@@ -388,7 +394,7 @@
         [ext_slope * ext_g * ext_cos, -ext_g * ext_imag, jnp.zeros((6, ROWS), F32)], 0
     )
     acc_ghbe[...] += ext_grads
-    acc_ghwe[...] += dot3(split(ext_grads), res)
+    acc_ghwe[...] += dot3_few(ext_grads, res)
     gl = (gl_h[...], gl_l[...])
     ext_cols = ext_grads.T
     grad_mixed = (

time: 283 us -> 281 us (level)
  transfers between devices with their start and end apart: 42 -> 42, of which waited for: 8 -> 8; matrix products, arithmetic and copies ran while one was open for 4% -> 4% of each run, Pallas kernels for 36% -> 37%
where the time goes in v2:
time: 281 us; the launch traced here: 280 us
  Pallas kernels  199 us (71%)
  starting transfers between devices  43.1 us (15%)
  other arithmetic  18.6 us (7%)
  waiting for transfers between devices  13 us (5%)
  local copies, waits for them, and re-layouts  4.45 us (2%)
    pallas_call x1, Pallas kernels, run_head(): pl.pallas_call(head_kernel, grid_spec=pltpu.PrefetchScalarGridSpec(num_sc...  94.8 us
    pallas_call x2, Pallas kernels, run_up(): pl.pallas_call(up_kernel, grid=(count // rows,), in_specs=in_specs + [pl....  33.7 us
    pallas_call x2, Pallas kernels, run_norm(): pl.pallas_call(functools.partial(norm_kernel, [pair[0].shape[1] for pair...  23.1 us
    ppermute x28, starting transfers between devices, exchange(): lax.ppermute(value, 'clip', [(i, i ^ across['clip']) for i in range(lax.a...  22.7 us
    pallas_call x2, Pallas kernels, run_wave(): pl.pallas_call(functools.partial(wave_kernel, first_blk, count // clips,...  19.9 us
    pallas_call x2, Pallas kernels, run_conv(): pl.pallas_call(functools.partial(conv_kernel, clip), grid_spec=pltpu.Pref...  13.8 us
    add x8, other arithmetic, added(): sum((lax.dynamic_slice(v, (row, col), (rows, cols)) for v, row, col in te...  13.4 us
    ppermute x10, starting transfers between devices, exchange(): lax.ppermute(value, 'tm', [(i, i ^ across['tm']) for i in range(lax.axis_...  11.8 us
  transfers between devices with their start and end apart: 42, of which 8 were waited for; matrix products, arithmetic and copies ran while one was open for 4% of the time, Pallas kernels for 37%

profile of v2, /device:TPU:0, one launch (start us, length us, event | category | flops | bytes accessed | tf_op | source)
XLA Modules:
  0.0 279.5 jit_solution(7725472130270759428)
XLA Ops:
  1.4 3.0 %collective-permute-start.1 = (f32[2,8,640]{2,1,0:T(8,128)S(1)}, f32[2,8,640]{2,1,0:T(8,128)S(1)}, u32[]{:S(2)}, u32[]{:S(2)}) collective-permute-start(f32[2,8,640]{2,1,0:T(8,128)S(1)} %pad.4), channel_id=1, source_target_pairs={{0,1},{1,0},{2,3},{3,2},{4,5},{5,4},{6,7},{7,6},{8,9},{9,8},{10,11... | collective-permute-start | bytes 122888 | tf_op jit(solution)/shard_map/ppermute | solution.py:1164
  5.2 3.9 %collective-permute-done.edge_ref = f32[2,8,512]{2,1,0:T(8,128)S(1)} collective-permute-done((f32[2,8,512]{2,1,0:T(8,128)S(1)}, f32[2,8,512]{2,1,0:T(8,128)S(1)}, u32[]{:S(2)}, u32[]{:S(2)}) %collective-permute-start) | collective-permute-done | bytes 32800 | tf_op jit(solution)/shard_map/ppermute | solution.py:1164
  9.7 94.8 %head.1 = (f32[2048,512]{1,0:T(8,128)}, f32[2048,128]{1,0:T(8,128)}, bf16[512,2048]{1,0:T(8,128)(2,1)}, bf16[512,2048]{1,0:T(8,128)(2,1)}, f32[2048,1536]{1,0:T(...) custom-call(s32[2]{0:T(128)} %bands.5, s32[2]{0:T(128)} %offsets.9, ...), custom_call_target="tpu_custom_call" | custom-call | flops 80000000000 | bytes 90000000 | tf_op jit(solution)/shard_map/head/pallas_call | solution.py:541
  104.7 5.6 %collective-permute-done.2 = f32[1472,512]{1,0:T(8,128)S(1)} collective-permute-done((f32[1472,512]{1,0:T(8,128)}, f32[1472,512]{1,0:T(8,128)S(1)}, u32[]{:S(2)}, u32[]{:S(2)}) %collective-permute-start.2) | collective-permute-done | bytes 3014688 | tf_op jit(solution)/shard_map/ppermute | solution.py:923
  110.3 3.8 %dynamic-slice_add_fusion = (f32[736,256]{1,0:T(8,128)}, f32[736,256]{1,0:T(8,128)}) fusion(f32[1472,512]{1,0:T(8,128)S(1)} %collective-permute-done.2, s32[]{:T(128)S(6)} %select_n.186, f32[1472,512]{1,0:T(8,128)} %get-tuple-element.142, s32[]{:T(128)S(6)} %select_n.185), kind=kLoop, calls=%fused_computation.8 | loop fusion | flops 376832 | bytes 4521992 | tf_op jit(solution)/shard_map/add | solution.py:996
  114.1 1.5 collective-permute-start.3
  116.1 21.2 %up_grads.2 = (f32[768,512]{1,0:T(8,128)}, f32[768,512]{1,0:T(8,128)}, f32[1,1024]{1,0:T(1,128)}, bf16[2048,1024]{1,0:T(8,128)(2,1)}, bf16[2048,1024]{1,0:T(8,128)(2,1)}) custom-call(bf16[2048,512]{1,0:T(8,128)(2,1)} %get-tuple-element.144.gb_h, bf16[2048,512]{1,0:T(8,128)(2,1)} %get-tuple-element.145.gb_l, f32[2048,1536]{1,0:T(8,128)} %get-tuple-element.157.slope, ...), custom_call_target="tpu_custom_call" | custom-call | flops 10000000000 | bytes 20000000 | tf_op jit(solution)/shard_map/up_grads/pallas_call | solution.py:599
  137.4 1.5 dynamic-slice_add_fusion.4
  138.9 1.6 collective-permute-start.5
  141.0 12.5 %up_grads.3 = (f32[768,512]{1,0:T(8,128)}, f32[768,512]{1,0:T(8,128)}, f32[1,512]{1,0:T(1,128)}, bf16[2048,512]{1,0:T(8,128)(2,1)}, bf16[2048,512]{1,0:T(8,128)(2,1)}) custom-call(bf16[2048,512]{1,0:T(8,128)(2,1)} %get-tuple-element.144.gb_h, bf16[2048,512]{1,0:T(8,128)(2,1)} %get-tuple-element.145.gb_l, ...), custom_call_target="tpu_custom_call", output_to_operand_aliasing={{0}: (6, {}), {1}: (7, {})} | custom-call | flops 10000000000 | bytes 20000000 | tf_op jit(solution)/shard_map/up_grads/pallas_call | solution.py:599
  153.8 1.9 add_add_fusion
  155.7 0.9 fusion
  156.5 1.6 collective-permute-start.7
  158.1 1.2 dynamic-slice_add_fusion.2
  159.9 1.5 collective-permute-start.9
  161.4 11.6 %norm_grads.2 = (f32[1024,512]{1,0:T(8,128)}, f32[2,8,512]{2,1,0:T(8,128)}, f32[4,512]{1,0:T(4,128)}, f32[4,512]{1,0:T(4,128)}) custom-call(s32[2]{0:T(128)} %bands.5, bf16[2048,1024]{1,0:T(8,128)(2,1)} %get-tuple-element.169.refs_0_, bf16[2048,1024]{1,0:T(8,128)(2,1)} %get-tuple-element.170.refs_1_, bf16[2048,512]{1,0:T(8,128)(2,1)} %get-tuple-element.171.refs_2_, ...), custom_call_target="tpu_custom_call" | custom-call | flops 5000000000 | bytes 12000000 | tf_op jit(solution)/shard_map/norm_grads/pallas_call | solution.py:682
  173.1 1.1 dynamic-slice_add_fusion.6
  174.2 1.6 collective-permute-start.12
  176.3 1.7 fusion.2
  177.9 2.6 collective-permute-start.11
  180.5 11.5 %norm_grads.3 = (f32[1024,512]{1,0:T(8,128)}, f32[2,8,512]{2,1,0:T(8,128)}, f32[4,512]{1,0:T(4,128)}, f32[4,512]{1,0:T(4,128)}) custom-call(s32[2]{0:T(128)} %bands.5, bf16[2048,1024]{1,0:T(8,128)(2,1)} %get-tuple-element.169.refs_0_, bf16[2048,1024]{1,0:T(8,128)(2,1)} %get-tuple-element.170.refs_1_, bf16[2048,512]{1,0:T(8,128)(2,1)} %get-tuple-element.171.refs_2_, ...), custom_call_target="tpu_custom_call" | custom-call | flops 5000000000 | bytes 12000000 | tf_op jit(solution)/shard_map/norm_grads/pallas_call | solution.py:682
  192.1 1.1 add_add_fusion.3
  193.2 0.8 collective-permute-start.15
  194.1 1.1 fusion.5
  196.1 10.0 %wave.2 = (f32[5120,128]{1,0:T(8,128)}, f32[2,8,640]{2,1,0:T(8,128)}) custom-call(s32[2]{0:T(128)} %offsets.9, f32[2048,1280]{1,0:T(8,128)} %get-tuple-element.223.spec, bf16[512,512]{1,0:T(8,128)(2,1)} %constant.144.clone.t1h, bf16[512,512]{1,0:T(8,128)(2,1)} %constant.145.clone.t1l, bf16[512,512]{1,0:T(8,128)(2,1)} %constant.146.clone.t2h, ...), custom_call_target="tpu_custom_call" | custom-call | flops 5000000000 | bytes 8000000 | tf_op jit(solution)/shard_map/wave/pallas_call | solution.py:890
  206.1 0.8 collective-permute-done.15
  207.6 3.4 %collective-permute-start.18 = (f32[2,8,640]{2,1,0:T(8,128)S(1)}, f32[2,8,640]{2,1,0:T(8,128)S(1)}, u32[]{:S(2)}, u32[]{:S(2)}) collective-permute-start(f32[2,8,640]{2,1,0:T(8,128)S(1)} %copy-done.20), channel_id=1, source_target_pairs={{0,1},{2,3},{4,5},{6,7},{8,9},{10,11},{12,13},{14,15},{16,17},{18,... | collective-permute-start | bytes 122888 | tf_op jit(solution)/shard_map/ppermute | solution.py:918
  211.0 2.7 collective-permute-start.21
  213.7 6.7 %conv_grads.2 = (f32[2,1024,512]{2,1,0:T(8,128)}, f32[64,512]{1,0:T(8,128)}) custom-call(s32[2]{0:T(128)} %offsets.9, f32[2,1024,512]{2,1,0:T(8,128)} %x_down.5, f32[2,1024,512]{2,1,0:T(8,128)} %x_down.5, f32[2,1024,512]{2,1,0:T(8,128)} %x_down.5, f32[2,8,512]{2,1,0:T(8,128)} %copy-done.17, f32[1,1024,512]{2,1,0:T(8,128)} %bitcast.16, ...), custom_call_target="tpu_custom_call" | custom-call | flops 5000000000 | bytes 17000000 | tf_op jit(solution)/shard_map/conv_grads/pallas_call | solution.py:772
  220.8 2.9 %collective-permute-start.19 = (f32[368,256]{1,0:T(8,128)S(1)}, f32[368,256]{1,0:T(8,128)S(1)}, u32[]{:S(2)}, u32[]{:S(2)}) collective-permute-start(f32[368,256]{1,0:T(8,128)S(1)} %get-tuple-element.284), channel_id=1, source_target_pairs={{0,1},{1,0},{2,3},{3,2},{4,5},{5,4},{6,7},{7,6},{8,9},{9,8},{10,11... | collective-permute-start | bytes 1130504 | tf_op jit(solution)/shard_map/ppermute | solution.py:925
  223.6 1.5 collective-permute-start.20
  225.1 7.1 %conv_grads.3 = (f32[2,1024,512]{2,1,0:T(8,128)}, f32[64,512]{1,0:T(8,128)}) custom-call(s32[2]{0:T(128)} %offsets.9, f32[2,1024,512]{2,1,0:T(8,128)} %x_down.5, f32[2,1024,512]{2,1,0:T(8,128)} %x_down.5, f32[2,1024,512]{2,1,0:T(8,128)} %x_down.5, f32[2,8,512]{2,1,0:T(8,128)} %copy-done.17, ...), custom_call_target="tpu_custom_call", output_to_operand_aliasing={{0}: (12, {})} | custom-call | flops 5000000000 | bytes 17000000 | tf_op jit(solution)/shard_map/conv_grads/pallas_call | solution.py:772
  232.5 2.5 collective-permute-start.22
  235.0 1.6 pack.1
  236.7 2.0 collective-permute-start.24
  238.7 0.8 add.328
  239.6 2.1 collective-permute-start.27
  241.7 9.9 %wave.3 = (f32[5120,128]{1,0:T(8,128)}, f32[2,8,640]{2,1,0:T(8,128)}) custom-call(s32[2]{0:T(128)} %offsets.9, f32[2048,1280]{1,0:T(8,128)} %get-tuple-element.223.spec, bf16[512,512]{1,0:T(8,128)(2,1)} %constant.144.clone.t1h, bf16[512,512]{1,0:T(8,128)(2,1)} %constant.145.clone.t1l, ...), custom_call_target="tpu_custom_call", output_to_operand_aliasing={{0}: (11, {})} | custom-call | flops 5000000000 | bytes 8000000 | tf_op jit(solution)/shard_map/wave/pallas_call | solution.py:890
  251.5 1.5 collective-permute-done.27
  254.8 1.0 pad_maximum_fusion.3.refs_0_
  255.8 1.4 collective-permute-start.28
  257.4 1.5 collective-permute-start.30
  258.9 2.0 collective-permute-start.32
  261.0 0.8 slice.23
  261.8 5.8 %in_order.2 = (f32[1282,512]{1,0:T(8,128)}, f32[1536,512]{1,0:T(8,128)}) custom-call(f32[736,256]{1,0:T(8,128)} %copy-done.3, f32[736,256]{1,0:T(8,128)} %collective-permute-done.22.refs_1_, f32[736,256]{1,0:T(8,128)} %copy-done.2, f32[736,256]{1,0:T(8,128)} %copy-done.8, f32[736,256]{1,0:T(8,128)} %copy-done.9, f32[736,256]{1,0:T(8,128)} %copy-done.10, ...), custom_call_target="tpu_custom_call" | custom-call | tf_op jit(solution)/shard_map/in_order/pallas_call | solution.py:1102
  270.4 1.3 dynamic_update_slice.3
  272.7 4.7 %in_order.3 = f32[512,1536]{1,0:T(8,128)} custom-call(f32[384,256]{1,0:T(8,128)} %copy-done.5, f32[384,256]{1,0:T(8,128)} %copy-done.14, f32[384,256]{1,0:T(8,128)} %copy-done.4, f32[384,256]{1,0:T(8,128)} %copy-done.13, f32[384,256]{1,0:T(8,128)} %copy-done.15, f32[384,256]{1,0:T(8,128)} %copy-done.16, f32[384,256]{1,0:T(8,128)} %collective-permute-done.40.refs_6_, ...), custom_call_target="tpu_custom_call" | custom-call | tf_op jit(solution)/shard_map/in_order/pallas_call | solution.py:1102
  278.0 1.5 unpack.1
  (129 shorter events, 13.0 us)
Async XLA Ops:
  1.4 7.7 %collective-permute-start.1 = (f32[2,8,640]{2,1,0:T(8,128)S(1)}, f32[2,8,640]{2,1,0:T(8,128)S(1)}, u32[]{:S(2)}, u32[]{:S(2)}) collective-permute-start(f32[2,8,640]{2,1,0:T(8,128)S(1)} %pad.4), channel_id=1, source_target_pairs={{0,1},{1,0},{2,3},{3,2},{4,5},{5,4},{6,7},{7,6},{8,9},{9,8},{10,11... | collective-permute-start | bytes 122888 | tf_op jit(solution)/shard_map/ppermute | solution.py:1164
  5.2 3.9 %collective-permute-start = (f32[2,8,512]{2,1,0:T(8,128)S(1)}, f32[2,8,512]{2,1,0:T(8,128)S(1)}, u32[]{:S(2)}, u32[]{:S(2)}) collective-permute-start(f32[2,8,512]{2,1,0:T(8,128)S(1)} %slice_select_fusion), channel_id=1, source_target_pairs={{0,1},{1,0},{2,3},{3,2},{4,5},{5,4},{6,7},{7,6},{8,9},{9,8},{10,11... | collective-permute-start | bytes 98312 | tf_op jit(solution)/shard_map/ppermute | solution.py:1164
  104.6 5.7 %collective-permute-start.2 = (f32[1472,512]{1,0:T(8,128)}, f32[1472,512]{1,0:T(8,128)S(1)}, u32[]{:S(2)}, u32[]{:S(2)}) collective-permute-start(f32[1472,512]{1,0:T(8,128)} %get-tuple-element.143), channel_id=1, source_target_pairs={{0,2},{2,0},{4,6},{6,4},{8,10},{10,8},{12,14},{14,12},{16,18},{18,... | collective-permute-start | bytes 9043976 | tf_op jit(solution)/shard_map/ppermute | solution.py:923
  114.1 23.2 %collective-permute-start.3 = (f32[736,256]{1,0:T(8,128)}, f32[736,256]{1,0:T(8,128)}, u32[]{:S(2)}, u32[]{:S(2)}) collective-permute-start(f32[736,256]{1,0:T(8,128)} %get-tuple-element.276), channel_id=1, source_target_pairs={{0,4},{2,6},{4,0},{6,2},{8,12},{10,14},{12,8},{14,10},{16,20},{18,... | collective-permute-start | bytes 2261000 | tf_op jit(solution)/shard_map/ppermute | solution.py:923
  115.6 21.7 %collective-permute-start.4 = (f32[736,256]{1,0:T(8,128)}, f32[736,256]{1,0:T(8,128)}, u32[]{:S(2)}, u32[]{:S(2)}) collective-permute-start(f32[736,256]{1,0:T(8,128)} %get-tuple-element.275), channel_id=1, source_target_pairs={{0,1},{1,0},{2,3},{3,2},{4,5},{5,4},{6,7},{7,6},{8,9},{9,8},{10,11... | collective-permute-start | bytes 2261000 | tf_op jit(solution)/shard_map/ppermute | solution.py:925
  116.1 21.2 %copy-start = (f32[1472,512]{1,0:T(8,128)S(1)}, f32[1472,512]{1,0:T(8,128)}, u32[]{:S(2)}) copy-start(f32[1472,512]{1,0:T(8,128)} %get-tuple-element.142) | copy-start | bytes 9043972
  138.9 14.6 %collective-permute-start.5 = (f32[368,256]{1,0:T(8,128)S(1)}, f32[368,256]{1,0:T(8,128)}, u32[]{:S(2)}, u32[]{:S(2)}) collective-permute-start(f32[368,256]{1,0:T(8,128)S(1)} %get-tuple-element.274), channel_id=1, source_target_pairs={{0,1},{1,0},{2,3},{3,2},{4,5},{5,4},{6,7},{7,6},{8,9},{9,8},{10,11... | collective-permute-start | bytes 1130504 | tf_op jit(solution)/shard_map/ppermute | solution.py:925
  140.4 13.0 %collective-permute-start.6 = (f32[368,256]{1,0:T(8,128)S(1)}, f32[368,256]{1,0:T(8,128)}, u32[]{:S(2)}, u32[]{:S(2)}) collective-permute-start(f32[368,256]{1,0:T(8,128)S(1)} %get-tuple-element.273), channel_id=1, source_target_pairs={{0,4},{2,6},{4,0},{6,2},{8,12},{10,14},{12,8},{14,10},{16,20},{18,... | collective-permute-start | bytes 1130504 | tf_op jit(solution)/shard_map/ppermute | solution.py:923
  153.5 4.6 %collective-permute-start.8 = (f32[768,512]{1,0:T(8,128)}, f32[768,512]{1,0:T(8,128)}, u32[]{:S(2)}, u32[]{:S(2)}) collective-permute-start(f32[768,512]{1,0:T(8,128)} %get-tuple-element.168), channel_id=1, source_target_pairs={{0,2},{2,0},{4,6},{6,4},{8,10},{10,8},{12,14},{14,12},{16,18},{18,... | collective-permute-start | bytes 4718600 | tf_op jit(solution)/shard_map/ppermute | solution.py:923
  156.5 16.5 %collective-permute-start.7 = (f32[368,256]{1,0:T(8,128)}, f32[368,256]{1,0:T(8,128)}, u32[]{:S(2)}, u32[]{:S(2)}) collective-permute-start(f32[368,256]{1,0:T(8,128)} %fusion), channel_id=1, source_target_pairs={{0,8},{2,10},{4,12},{6,14},{8,0},{10,2},{12,4},{14,6},{16,24},{18,... | collective-permute-start | bytes 1130504 | tf_op jit(solution)/shard_map/ppermute | solution.py:923
  159.3 13.7 %collective-permute-start.10 = (f32[384,256]{1,0:T(8,128)S(1)}, f32[384,256]{1,0:T(8,128)S(1)}, u32[]{:S(2)}, u32[]{:S(2)}) collective-permute-start(f32[384,256]{1,0:T(8,128)S(1)} %get-tuple-element.281), channel_id=1, source_target_pairs={{0,1},{1,0},{2,3},{3,2},{4,5},{5,4},{6,7},{7,6},{8,9},{9,8},{10,11... | collective-permute-start | bytes 1179656 | tf_op jit(solution)/shard_map/ppermute | solution.py:925
  159.9 13.1 %collective-permute-start.9 = (f32[384,256]{1,0:T(8,128)S(1)}, f32[384,256]{1,0:T(8,128)S(1)}, u32[]{:S(2)}, u32[]{:S(2)}) collective-permute-start(f32[384,256]{1,0:T(8,128)S(1)} %get-tuple-element.282), channel_id=1, source_target_pairs={{0,4},{2,6},{4,0},{6,2},{8,12},{10,14},{12,8},{14,10},{16,20},{18,... | collective-permute-start | bytes 1179656 | tf_op jit(solution)/shard_map/ppermute | solution.py:923
  174.2 17.9 %collective-permute-start.12 = (f32[192,256]{1,0:T(8,128)S(1)}, f32[192,256]{1,0:T(8,128)S(1)}, u32[]{:S(2)}, u32[]{:S(2)}) collective-permute-start(f32[192,256]{1,0:T(8,128)S(1)} %get-tuple-element.280), channel_id=1, source_target_pairs={{0,1},{1,0},{2,3},{3,2},{4,5},{5,4},{6,7},{7,6},{8,9},{9,8},{10,11... | collective-permute-start | bytes 589832 | tf_op jit(solution)/shard_map/ppermute | solution.py:925
  175.7 16.3 %collective-permute-start.13 = (f32[192,256]{1,0:T(8,128)S(1)}, f32[192,256]{1,0:T(8,128)S(1)}, u32[]{:S(2)}, u32[]{:S(2)}) collective-permute-start(f32[192,256]{1,0:T(8,128)S(1)} %get-tuple-element.279), channel_id=1, source_target_pairs={{0,4},{2,6},{4,0},{6,2},{8,12},{10,14},{12,8},{14,10},{16,20},{18,... | collective-permute-start | bytes 589832 | tf_op jit(solution)/shard_map/ppermute | solution.py:923
  177.9 14.1 %collective-permute-start.11 = (f32[184,256]{1,0:T(8,128)}, f32[184,256]{1,0:T(8,128)}, u32[]{:S(2)}, u32[]{:S(2)}) collective-permute-start(f32[184,256]{1,0:T(8,128)} %fusion.2), channel_id=1, source_target_pairs={{0,16},{2,18},{4,20},{6,22},{8,24},{10,26},{12,28},{14,30},{16,0},... | collective-permute-start | bytes 565256 | tf_op jit(solution)/shard_map/ppermute | solution.py:923
  193.2 13.7 %collective-permute-start.15 = (f32[384,256]{1,0:T(8,128)S(1)}, f32[384,256]{1,0:T(8,128)S(1)}, u32[]{:S(2)}, u32[]{:S(2)}) collective-permute-start(f32[384,256]{1,0:T(8,128)S(1)} %pad_maximum_fusion.2), channel_id=1, source_target_pairs={{0,8},{2,10},{4,12},{6,14},{8,0},{10,2},{12,4},{14,6},{16,24},{18,... | collective-permute-start | bytes 1179656 | tf_op jit(solution)/shard_map/ppermute | solution.py:923
  195.2 10.9 %collective-permute-start.14 = (f32[184,256]{1,0:T(8,128)S(1)}, f32[184,256]{1,0:T(8,128)S(1)}, u32[]{:S(2)}, u32[]{:S(2)}) collective-permute-start(f32[184,256]{1,0:T(8,128)S(1)} %fusion.5), channel_id=1, source_target_pairs={{0,16},{2,18},{4,20},{6,22},{8,24},{10,26},{12,28},{14,30},{16,0},... | collective-permute-start | bytes 565256 | tf_op jit(solution)/shard_map/ppermute | solution.py:923
  195.6 10.5 %collective-permute-start.16 = (f32[2,8,512]{2,1,0:T(8,128)S(1)}, f32[2,8,512]{2,1,0:T(8,128)S(1)}, u32[]{:S(2)}, u32[]{:S(2)}) collective-permute-start(f32[2,8,512]{2,1,0:T(8,128)S(1)} %copy-done.22), channel_id=1, source_target_pairs={{0,1},{1,0},{2,3},{3,2},{4,5},{5,4},{6,7},{7,6},{8,9},{9,8},{10,11... | collective-permute-start | bytes 98312 | tf_op jit(solution)/shard_map/ppermute | solution.py:925
  207.1 13.6 %collective-permute-start.17 = (f32[368,256]{1,0:T(8,128)S(1)}, f32[368,256]{1,0:T(8,128)S(1)}, u32[]{:S(2)}, u32[]{:S(2)}) collective-permute-start(f32[368,256]{1,0:T(8,128)S(1)} %pad_maximum_fusion.5), channel_id=1, source_target_pairs={{0,8},{2,10},{4,12},{6,14},{8,0},{10,2},{12,4},{14,6},{16,24},{18,... | collective-permute-start | bytes 1130504 | tf_op jit(solution)/shard_map/ppermute | solution.py:923
  207.6 12.8 %collective-permute-start.18 = (f32[2,8,640]{2,1,0:T(8,128)S(1)}, f32[2,8,640]{2,1,0:T(8,128)S(1)}, u32[]{:S(2)}, u32[]{:S(2)}) collective-permute-start(f32[2,8,640]{2,1,0:T(8,128)S(1)} %copy-done.20), channel_id=1, source_target_pairs={{0,1},{2,3},{4,5},{6,7},{8,9},{10,11},{12,13},{14,15},{16,17},{18,... | collective-permute-start | bytes 122888 | tf_op jit(solution)/shard_map/ppermute | solution.py:918
  211.0 21.2 %collective-permute-start.21 = (f32[384,256]{1,0:T(8,128)S(1)}, f32[384,256]{1,0:T(8,128)S(1)}, u32[]{:S(2)}, u32[]{:S(2)}) collective-permute-start(f32[384,256]{1,0:T(8,128)S(1)} %fusion.6), channel_id=1, source_target_pairs={{0,16},{2,18},{4,20},{6,22},{8,24},{10,26},{12,28},{14,30},{16,0},... | collective-permute-start | bytes 1179656 | tf_op jit(solution)/shard_map/ppermute | solution.py:923
  220.4 11.8 %copy-start.19 = (f32[2,8,640]{2,1,0:T(8,128)}, f32[2,8,640]{2,1,0:T(8,128)S(1)}, u32[]{:S(2)}) copy-start(f32[2,8,640]{2,1,0:T(8,128)S(1)} %collective-permute-done.18.refs_0_) | copy-start | bytes 122884
  220.8 11.4 %collective-permute-start.19 = (f32[368,256]{1,0:T(8,128)S(1)}, f32[368,256]{1,0:T(8,128)S(1)}, u32[]{:S(2)}, u32[]{:S(2)}) collective-permute-start(f32[368,256]{1,0:T(8,128)S(1)} %get-tuple-element.284), channel_id=1, source_target_pairs={{0,1},{1,0},{2,3},{3,2},{4,5},{5,4},{6,7},{7,6},{8,9},{9,8},{10,11... | collective-permute-start | bytes 1130504 | tf_op jit(solution)/shard_map/ppermute | solution.py:925
  223.6 8.7 %collective-permute-start.20 = (f32[368,256]{1,0:T(8,128)S(1)}, f32[368,256]{1,0:T(8,128)S(1)}, u32[]{:S(2)}, u32[]{:S(2)}) collective-permute-start(f32[368,256]{1,0:T(8,128)S(1)} %get-tuple-element.283), channel_id=1, source_target_pairs={{0,4},{2,6},{4,0},{6,2},{8,12},{10,14},{12,8},{14,10},{16,20},{18,... | collective-permute-start | bytes 1130504 | tf_op jit(solution)/shard_map/ppermute | solution.py:923
  232.3 21.3 %copy-start.2 = (f32[736,256]{1,0:T(8,128)}, f32[736,256]{1,0:T(8,128)S(1)}, u32[]{:S(2)}) copy-start(f32[736,256]{1,0:T(8,128)S(1)} %pad_maximum_fusion.1.refs_2_) | copy-start | bytes 2260996
  232.4 20.6 %copy-start.3 = (f32[736,256]{1,0:T(8,128)}, f32[736,256]{1,0:T(8,128)S(1)}, u32[]{:S(2)}) copy-start(f32[736,256]{1,0:T(8,128)S(1)} %pad_maximum_fusion.refs_0_) | copy-start | bytes 2260996
  232.4 20.6 %collective-permute-start.23 = (f32[736,256]{1,0:T(8,128)S(1)}, f32[736,256]{1,0:T(8,128)S(1)}, u32[]{:S(2)}, u32[]{:S(2)}) collective-permute-start(f32[736,256]{1,0:T(8,128)S(1)} %pad_maximum_fusion.1.refs_2_), channel_id=1, source_target_pairs={{0,1},{1,0},{2,3},{3,2},{4,5},{5,4},{6,7},{7,6},{8,9},{9,8},{10,11... | collective-permute-start | bytes 2261000 | tf_op jit(solution)/shard_map/ppermute | solution.py:925
  232.5 20.5 %collective-permute-start.22 = (f32[736,256]{1,0:T(8,128)S(1)}, f32[736,256]{1,0:T(8,128)}, u32[]{:S(2)}, u32[]{:S(2)}) collective-permute-start(f32[736,256]{1,0:T(8,128)S(1)} %pad_maximum_fusion.refs_0_), channel_id=1, source_target_pairs={{0,4},{2,6},{4,0},{6,2},{8,12},{10,14},{12,8},{14,10},{16,20},{18,... | collective-permute-start | bytes 2261000 | tf_op jit(solution)/shard_map/ppermute | solution.py:923
  236.6 2.1 collective-permute-start.26
  236.7 16.3 %collective-permute-start.24 = (f32[192,256]{1,0:T(8,128)S(1)}, f32[192,256]{1,0:T(8,128)}, u32[]{:S(2)}, u32[]{:S(2)}) collective-permute-start(f32[192,256]{1,0:T(8,128)S(1)} %get-tuple-element.286), channel_id=1, source_target_pairs={{0,1},{1,0},{2,3},{3,2},{4,5},{5,4},{6,7},{7,6},{8,9},{9,8},{10,11... | collective-permute-start | bytes 589832 | tf_op jit(solution)/shard_map/ppermute | solution.py:925
  238.7 14.3 %collective-permute-start.25 = (f32[192,256]{1,0:T(8,128)S(1)}, f32[192,256]{1,0:T(8,128)S(1)}, u32[]{:S(2)}, u32[]{:S(2)}) collective-permute-start(f32[192,256]{1,0:T(8,128)S(1)} %get-tuple-element.285), channel_id=1, source_target_pairs={{0,4},{2,6},{4,0},{6,2},{8,12},{10,14},{12,8},{14,10},{16,20},{18,... | collective-permute-start | bytes 589832 | tf_op jit(solution)/shard_map/ppermute | solution.py:923
  239.6 13.4 %collective-permute-start.27 = (f32[32,512]{1,0:T(8,128)S(1)}, f32[32,512]{1,0:T(8,128)S(1)}, u32[]{:S(2)}, u32[]{:S(2)}) collective-permute-start(f32[32,512]{1,0:T(8,128)S(1)} %add.328), channel_id=1, source_target_pairs={{0,4},{2,6},{4,0},{6,2},{8,12},{10,14},{12,8},{14,10},{16,20},{18,... | collective-permute-start | bytes 196616 | tf_op jit(solution)/shard_map/ppermute | solution.py:923
  253.0 2.7 collective-permute-start.33
  253.1 4.3 %collective-permute-start.34 = (f32[736,256]{1,0:T(8,128)}, f32[736,256]{1,0:T(8,128)S(1)}, u32[]{:S(2)}, u32[]{:S(2)}) collective-permute-start(f32[736,256]{1,0:T(8,128)} %collective-permute-done.22.refs_1_), channel_id=1, source_target_pairs={{0,2},{2,0},{4,6},{6,4},{8,10},{10,8},{12,14},{14,12},{16,18},{18,... | collective-permute-start | bytes 2261000 | tf_op jit(solution)/shard_map/ppermute | solution.py:923
  253.6 5.3 %collective-permute-start.35 = (f32[736,256]{1,0:T(8,128)S(1)}, f32[736,256]{1,0:T(8,128)S(1)}, u32[]{:S(2)}, u32[]{:S(2)}) collective-permute-start(f32[736,256]{1,0:T(8,128)S(1)} %pad_maximum_fusion.1.refs_2_), channel_id=1, source_target_pairs={{0,2},{2,0},{4,6},{6,4},{8,10},{10,8},{12,14},{14,12},{16,18},{18,... | collective-permute-start | bytes 2261000 | tf_op jit(solution)/shard_map/ppermute | solution.py:923
  253.7 5.2 %collective-permute-start.36 = (f32[736,256]{1,0:T(8,128)S(1)}, f32[736,256]{1,0:T(8,128)S(1)}, u32[]{:S(2)}, u32[]{:S(2)}) collective-permute-start(f32[736,256]{1,0:T(8,128)S(1)} %collective-permute-done.23.refs_3_), channel_id=1, source_target_pairs={{0,2},{2,0},{4,6},{6,4},{8,10},{10,8},{12,14},{14,12},{16,18},{18,... | collective-permute-start | bytes 2261000 | tf_op jit(solution)/shard_map/ppermute | solution.py:923
  254.2 14.6 %copy-start.4 = (f32[384,256]{1,0:T(8,128)}, f32[384,256]{1,0:T(8,128)S(1)}, u32[]{:S(2)}) copy-start(f32[384,256]{1,0:T(8,128)S(1)} %pad_maximum_fusion.4.refs_2_) | copy-start | bytes 1179652
  254.2 14.0 %collective-permute-start.29 = (f32[384,256]{1,0:T(8,128)S(1)}, f32[384,256]{1,0:T(8,128)S(1)}, u32[]{:S(2)}, u32[]{:S(2)}) collective-permute-start(f32[384,256]{1,0:T(8,128)S(1)} %pad_maximum_fusion.4.refs_2_), channel_id=1, source_target_pairs={{0,1},{1,0},{2,3},{3,2},{4,5},{5,4},{6,7},{7,6},{8,9},{9,8},{10,11... | collective-permute-start | bytes 1179656 | tf_op jit(solution)/shard_map/ppermute | solution.py:925
  255.7 12.4 %copy-start.5 = (f32[384,256]{1,0:T(8,128)}, f32[384,256]{1,0:T(8,128)S(1)}, u32[]{:S(2)}) copy-start(f32[384,256]{1,0:T(8,128)S(1)} %pad_maximum_fusion.3.refs_0_) | copy-start | bytes 1179652
  255.8 12.4 %collective-permute-start.28 = (f32[384,256]{1,0:T(8,128)S(1)}, f32[384,256]{1,0:T(8,128)S(1)}, u32[]{:S(2)}, u32[]{:S(2)}) collective-permute-start(f32[384,256]{1,0:T(8,128)S(1)} %pad_maximum_fusion.3.refs_0_), channel_id=1, source_target_pairs={{0,4},{2,6},{4,0},{6,2},{8,12},{10,14},{12,8},{14,10},{16,20},{18,... | collective-permute-start | bytes 1179656 | tf_op jit(solution)/shard_map/ppermute | solution.py:923
  257.4 10.7 %collective-permute-start.30 = (f32[32,512]{1,0:T(8,128)S(1)}, f32[32,512]{1,0:T(8,128)S(1)}, u32[]{:S(2)}, u32[]{:S(2)}) collective-permute-start(f32[32,512]{1,0:T(8,128)S(1)} %add.330), channel_id=1, source_target_pairs={{0,1},{1,0},{2,3},{3,2},{4,5},{5,4},{6,7},{7,6},{8,9},{9,8},{10,11... | collective-permute-start | bytes 196616 | tf_op jit(solution)/shard_map/ppermute | solution.py:925
  258.9 9.2 %collective-permute-start.31 = (f32[32,512]{1,0:T(8,128)S(1)}, f32[32,512]{1,0:T(8,128)S(1)}, u32[]{:S(2)}, u32[]{:S(2)}) collective-permute-start(f32[32,512]{1,0:T(8,128)S(1)} %add.330), channel_id=1, source_target_pairs={{0,8},{2,10},{4,12},{6,14},{8,0},{10,2},{12,4},{14,6},{16,24},{18,... | collective-permute-start | bytes 196616 | tf_op jit(solution)/shard_map/ppermute | solution.py:923
  258.9 9.2 %collective-permute-start.32 = (f32[32,512]{1,0:T(8,128)S(1)}, f32[32,512]{1,0:T(8,128)S(1)}, u32[]{:S(2)}, u32[]{:S(2)}) collective-permute-start(f32[32,512]{1,0:T(8,128)S(1)} %add.330), channel_id=1, source_target_pairs={{0,9},{1,8},{2,11},{3,10},{4,13},{5,12},{6,15},{7,14},{8,1},{9,0},... | collective-permute-start | bytes 196616 | tf_op jit(solution)/shard_map/ppermute | solution.py:928
  268.2 3.6 %collective-permute-start.38 = (f32[384,256]{1,0:T(8,128)S(1)}, f32[384,256]{1,0:T(8,128)S(1)}, u32[]{:S(2)}, u32[]{:S(2)}) collective-permute-start(f32[384,256]{1,0:T(8,128)S(1)} %pad_maximum_fusion.3.refs_0_), channel_id=1, source_target_pairs={{0,2},{2,0},{4,6},{6,4},{8,10},{10,8},{12,14},{14,12},{16,18},{18,... | collective-permute-start | bytes 1179656 | tf_op jit(solution)/shard_map/ppermute | solution.py:923
  268.3 3.5 %collective-permute-start.39 = (f32[384,256]{1,0:T(8,128)S(1)}, f32[384,256]{1,0:T(8,128)S(1)}, u32[]{:S(2)}, u32[]{:S(2)}) collective-permute-start(f32[384,256]{1,0:T(8,128)S(1)} %collective-permute-done.28.refs_1_), channel_id=1, source_target_pairs={{0,2},{2,0},{4,6},{6,4},{8,10},{10,8},{12,14},{14,12},{16,18},{18,... | collective-permute-start | bytes 1179656 | tf_op jit(solution)/shard_map/ppermute | solution.py:923
  268.8 3.0 %collective-permute-start.40 = (f32[384,256]{1,0:T(8,128)S(1)}, f32[384,256]{1,0:T(8,128)}, u32[]{:S(2)}, u32[]{:S(2)}) collective-permute-start(f32[384,256]{1,0:T(8,128)S(1)} %pad_maximum_fusion.4.refs_2_), channel_id=1, source_target_pairs={{0,2},{2,0},{4,6},{6,4},{8,10},{10,8},{12,14},{14,12},{16,18},{18,... | collective-permute-start | bytes 1179656 | tf_op jit(solution)/shard_map/ppermute | solution.py:923
  268.9 2.9 %collective-permute-start.41 = (f32[384,256]{1,0:T(8,128)S(1)}, f32[384,256]{1,0:T(8,128)}, u32[]{:S(2)}, u32[]{:S(2)}) collective-permute-start(f32[384,256]{1,0:T(8,128)S(1)} %collective-permute-done.29.refs_3_), channel_id=1, source_target_pairs={{0,2},{2,0},{4,6},{6,4},{8,10},{10,8},{12,14},{14,12},{16,18},{18,... | collective-permute-start | bytes 1179656 | tf_op jit(solution)/shard_map/ppermute | solution.py:923
  269.3 8.1 %collective-permute-start.37 = (f32[32,512]{1,0:T(8,128)S(1)}, f32[32,512]{1,0:T(8,128)S(1)}, u32[]{:S(2)}, u32[]{:S(2)}) collective-permute-start(f32[32,512]{1,0:T(8,128)S(1)} %add_add_fusion.4), channel_id=1, source_target_pairs={{0,16},{2,18},{4,20},{6,22},{8,24},{10,26},{12,28},{14,30},{16,0},... | collective-permute-start | bytes 196616 | tf_op jit(solution)/shard_map/ppermute | solution.py:923
  (17 other events, 64.2 us)
